TPU v7x, 512 devices: a whole 4x4x16 slice. The times are simulated.
512 devices in a mesh: graph: 128 (over z, x, core), mp: 4 (over y).
Axes of the slice: x: 4, y: 4, z: 16, core: 2. Of those that a mesh axis runs over, the one named last changes fastest.
Arguments:
- agents: float32 [32768, 256], P('graph'), may hold values from -30 to 30
- latents: float32 [64, 256], P(None, 'mp'), may hold values from -40 to 40
- w_local: float32 [256, 256], P(None, 'mp'), may hold values from -0.375 to 0.375
- w_value: float32 [256, 256], P(None, 'mp'), may hold values from -0.375 to 0.375
- w_up: float32 [256, 512], P(None, 'mp'), may hold values from -0.375 to 0.375
- w_down: float32 [512, 256], P('mp'), may hold values from -0.25 to 0.25
- neighbours: int32 [32768, 16], P('graph'), may hold values from 0 to 2303
- degree: int32 [32768], P('graph'), may hold values from 1 to 16
- send_rows: int32 [128, 128, 16], P('graph'), may hold values from 0 to 255
- cotangent: float32 [32768, 256], P('graph'), may hold values from -6 to 6
Outputs:
- updated: float32 [32768, 256], P('graph', 'mp')
- grad_agents: float32 [32768, 256], P('graph', 'mp')
- grad_latents: float32 [64, 256], P(None, 'mp')
- grad_local: float32 [256, 256], P(None, 'mp')
- grad_value: float32 [256, 256], P(None, 'mp')
- grad_up: float32 [256, 512], P(None, 'mp')
- grad_down: float32 [512, 256], P('mp')
All inputs are finite; a program needn't handle non-finite values.
Results may differ from a plain program's by a relative error of at most 0.0003.
Values sent between devices are 32-bit elements; how exact they have to be, the bound alone decides.
A program may use at most 64 MiB of HBM per device.

v0:
```python
import math

import jax
import jax.numpy as jnp
from jax import lax
from jax.sharding import PartitionSpec as P

HEAD_DIM = 64


HIGHEST = lax.Precision.HIGHEST


def matmul(left, right):
    return jnp.dot(left, right, precision=HIGHEST, preferred_element_type=jnp.float32)


def einsum_exact(form, left, right):
    return jnp.einsum(form, left, right, precision=HIGHEST)


def on_device(
    agents, latents, w_local, w_value, w_up, w_down, neighbours, degree, send_rows, cotangent
):
    row_count = agents.shape[0]
    col_count = latents.shape[1]
    vnode_count = latents.shape[0]
    graph_count = lax.axis_size("graph")
    column = lax.axis_index("mp")
    head_count = col_count // HEAD_DIM
    score_scale = 1.0 / math.sqrt(HEAD_DIM)
    agent_total = row_count * graph_count
    own_cols = lax.dynamic_slice_in_dim(agents, column * col_count, col_count, 1)
    own_cot = lax.dynamic_slice_in_dim(cotangent, column * col_count, col_count, 1)
    joined = jnp.concatenate([w_local, w_value], 1)
    projected = matmul(agents, joined)
    local_rows = projected[:, :col_count]
    values = projected[:, col_count:]
    outgoing = local_rows[send_rows[0]]
    incoming = lax.all_to_all(outgoing, "graph", split_axis=0, concat_axis=0, tiled=True)
    row_table = jnp.concatenate([local_rows, incoming.reshape(-1, col_count)], 0)
    slot_ids = jnp.arange(neighbours.shape[1], dtype=jnp.int32)
    slot_mask = (slot_ids[None, :] < degree[:, None]).astype(jnp.float32)
    degree_f = degree[:, None].astype(jnp.float32)
    message = jnp.sum(row_table[neighbours] * slot_mask[:, :, None], 1) / degree_f
    heads_x = own_cols.reshape(row_count, head_count, HEAD_DIM)
    heads_q = latents.reshape(vnode_count, head_count, HEAD_DIM)
    heads_v = values.reshape(row_count, head_count, HEAD_DIM)
    scores = einsum_exact("mhe,ahe->mha", heads_q, heads_x) * score_scale
    local_top = jnp.max(scores, -1)
    global_top = lax.pmax(local_top, "graph")
    weights = jnp.exp(scores - global_top[..., None])
    totals, weighted = lax.psum(
        (jnp.sum(weights, -1), einsum_exact("mha,ahe->mhe", weights, heads_v)), "graph"
    )
    prob = weights / totals[..., None]
    attended = weighted / totals[..., None]
    fresh = latents + attended.reshape(vnode_count, col_count)
    heads_f = fresh.reshape(vnode_count, head_count, HEAD_DIM)
    agent_scores = einsum_exact("ahe,mhe->ahm", heads_x, heads_f) * score_scale
    agent_prob = jax.nn.softmax(agent_scores, axis=-1)
    readout = einsum_exact("ahm,mhe->ahe", agent_prob, heads_f).reshape(row_count, col_count)
    hidden = own_cols + message + readout
    hidden_whole = lax.all_gather(hidden, "mp", axis=1, tiled=True)
    pre_act = matmul(hidden_whole, w_up)
    sigmoid_gate = jax.nn.sigmoid(pre_act)
    activated = pre_act * sigmoid_gate
    branch_out = lax.psum_scatter(matmul(activated, w_down), "mp", scatter_dimension=1, tiled=True)
    dpre_act = matmul(cotangent, w_down.T) * (sigmoid_gate * (1.0 + pre_act * (1.0 - sigmoid_gate)))
    grad_up = matmul(hidden_whole.T, dpre_act)
    grad_down = matmul(activated.T, cotangent)
    dhidden = own_cot + lax.psum_scatter(
        matmul(dpre_act, w_up.T), "mp", scatter_dimension=1, tiled=True
    )
    updated = hidden + branch_out
    dheads = dhidden.reshape(row_count, head_count, HEAD_DIM)
    dprob_agent = einsum_exact("ahe,mhe->ahm", dheads, heads_f)
    dagent = agent_prob * (dprob_agent - jnp.sum(agent_prob * dprob_agent, -1, keepdims=True))
    dx_heads = einsum_exact("ahm,mhe->ahe", dagent, heads_f) * score_scale
    dfresh_part = einsum_exact("ahm,ahe->mhe", dagent, heads_x) * score_scale + einsum_exact(
        "ahm,ahe->mhe", agent_prob, dheads
    )
    dfresh = lax.psum(dfresh_part, "graph")
    dvalues = einsum_exact("mha,mhe->ahe", prob, dfresh)
    dweights = einsum_exact("mhe,ahe->mha", dfresh, heads_v)
    centre = jnp.sum(dfresh * attended, -1)
    dscores = prob * (dweights - centre[..., None]) * score_scale
    dx_heads = dx_heads + einsum_exact("mha,mhe->ahe", dscores, heads_q)
    dlatent_part = einsum_exact("mha,ahe->mhe", dscores, heads_x)
    spread_grad = (dhidden / degree_f)[:, None, :] * slot_mask[:, :, None]
    dtable = jax.ops.segment_sum(
        spread_grad.reshape(-1, col_count), neighbours.reshape(-1), num_segments=row_table.shape[0]
    )
    returned = lax.all_to_all(
        dtable[row_count:].reshape(graph_count, -1, col_count),
        "graph",
        split_axis=0,
        concat_axis=0,
        tiled=True,
    )
    dlocal = dtable[:row_count] + jax.ops.segment_sum(
        returned.reshape(-1, col_count), send_rows[0].reshape(-1), num_segments=row_count
    )
    dprojected = jnp.concatenate([dlocal, dvalues.reshape(row_count, col_count)], 1)
    dthrough = lax.psum_scatter(matmul(dprojected, joined.T), "mp", scatter_dimension=1, tiled=True)
    grad_joined = matmul(agents.T, dprojected)
    grad_agents = dhidden + dx_heads.reshape(row_count, col_count) + dthrough
    summed = lax.psum((grad_joined, grad_up, grad_down, dlatent_part), "graph")
    factor = 1.0 / math.sqrt(agent_total)
    grad_latents = (
        dfresh.reshape(vnode_count, col_count) + summed[3].reshape(vnode_count, col_count)
    ) * factor
    grad_local = summed[0][:, :col_count] * factor
    grad_value = summed[0][:, col_count:] * factor
    return (
        updated,
        grad_agents,
        grad_latents,
        grad_local,
        grad_value,
        summed[1] * factor,
        summed[2] * factor,
    )


def solution(mesh):
    return jax.shard_map(
        on_device,
        mesh=mesh,
        in_specs=(
            P("graph", None),
            P(None, "mp"),
            P(None, "mp"),
            P(None, "mp"),
            P(None, "mp"),
            P("mp", None),
            P("graph", None),
            P("graph"),
            P("graph", None, None),
            P("graph", None),
        ),
        out_specs=(
            P("graph", "mp"),
            P("graph", "mp"),
            P(None, "mp"),
            P(None, "mp"),
            P(None, "mp"),
            P(None, "mp"),
            P("mp", None),
        ),
        check_vma=False,
    )
```

profile of v0, /device:TPU:1, one launch (start us, length us, event | category | flops | bytes accessed | tf_op | source)
XLA Modules:
  0.0 2284.6 jit_solution(16241532569100820926)
XLA Ops:
  7.2 0.7 compare_select_fusion.1
  7.9 0.1 copy.36
  8.1 0.8 constant_dynamic-update-slice_fusion.1
  9.0 0.8 constant_dynamic-update-slice_fusion
  9.8 1.3 convolution_bitcast_fusion.1
  11.3 5.5 gather_fusion
  16.8 1.4 reshape.265
  18.2 20.4 all-to-all-start
  38.7 0.6 convert_element_type.18
  39.4 0.1 copy.39
  39.6 0.1 constant_dynamic-slice_fusion.1
  39.7 0.7 copy.48
  40.4 0.4 fusion.47
  40.8 262.8 %pmax.7 = f32[64]{0:T(128)S(1)} all-reduce(f32[64]{0:T(128)S(1)} %get-tuple-element.37), channel_id=1, replica_groups=mesh['graph'=128,'mp'=4] {'graph'}, use_global_device_ids=true, to_apply=%region_2.0 | all-reduce | flops 64 | bytes 512 | tf_op jit(solution)/shard_map/pmax | solution.py:51
  303.6 0.2 fusion.30
  303.8 0.4 copy-done.31
  304.2 0.3 convolution_bitcast_fusion.8
  304.4 485.7 %all-reduce = (f32[64,1,64]{0,2,1:T(8,128)S(1)}, f32[64]{0:T(128)S(1)}) all-reduce(f32[64,1,64]{0,2,1:T(8,128)S(1)} %convolution_bitcast_fusion.8, f32[64]{0:T(128)S(1)} %fusion.30), channel_id=1, replica_groups=mesh['graph'=128,'mp'=4] {'graph'}, use_global_device_ids=true, to_apply=%region_3.0 | all-reduce | flops 4160 | bytes 33280 | tf_op jit(solution)/shard_map/psum | solution.py:53
  790.2 0.3 fusion.48
  790.5 0.6 fusion.28
  791.3 0.6 broadcast.101
  791.8 1.9 reduce.12
  793.8 0.3 reshape.266
  794.2 14.1 gather_fusion.1
  808.3 2.7 multiply_reduce_fusion
  811.2 0.2 fusion.9
  811.4 9.9 all_gather.3
  821.3 0.6 fusion.49
  822.0 0.4 convolution_multiply_fusion
  822.4 1.1 fusion.50
  823.5 0.1 copy.45
  823.7 0.1 copy.43
  823.9 0.1 constant_dynamic-slice_fusion
  824.2 1.1 fusion.37
  825.4 32.3 %reduce-scatter.6.cloned.1.call-done = f32[256,64]{0,1:T(8,128)} async-done(((f32[256,256]{0,1:T(8,128)}), f32[256,64]{0,1:T(8,128)}) %reduce-scatter.6.cloned.1.call-update) | async-done | bytes 65552 | tf_op jit(solution)/shard_map/reduce_scatter | solution.py:72
  857.6 1.5 broadcast_divide_fusion
  859.2 1.7 bitcast_multiply_fusion
  860.9 23.1 %scatter_custom_fusion = f32[2304,64]{1,0:T(8,128)S(1)} fusion(s32[4096]{0:T(1024)S(1)} %reshape.244, f32[4096,64]{1,0:T(8,128)} %bitcast_multiply_fusion, f32[]{:T(128)} %constant.15.clone.1), kind=kCustom, calls=%fused_computation.33 | custom fusion | flops 262144 | bytes 590336 | tf_op jit(solution)/shard_map/scatter-add | solution.py:91
  884.2 1.5 reshape.267
  885.7 19.0 all-to-all-start.1
  904.8 1.9 fusion.51
  906.7 2.0 fusion.35
  908.7 0.3 fusion.22
  909.0 0.4 convolution_multiply_fusion.4
  909.4 0.2 fusion.10
  909.6 499.0 %psum.51 = f32[64,1,64]{0,2,1:T(8,128)S(1)} all-reduce(f32[64,1,64]{0,2,1:T(8,128)S(1)} %fusion.10), channel_id=1, replica_groups=mesh['graph'=128,'mp'=4] {'graph'}, use_global_device_ids=true, to_apply=%region_11.0 | all-reduce | flops 4096 | bytes 32768 | tf_op jit(solution)/shard_map/psum | solution.py:83
  1408.7 0.3 fusion.8
  1408.9 0.4 convolution_bitcast_fusion.7
  1409.3 490.9 %psum.52 = f32[64,64]{0,1:T(8,128)S(1)} all-reduce(f32[64,64]{0,1:T(8,128)S(1)} %convolution_bitcast_fusion.7), channel_id=1, replica_groups=mesh['graph'=128,'mp'=4] {'graph'}, use_global_device_ids=true, to_apply=%region_16.0 | all-reduce | flops 4096 | bytes 32768 | tf_op jit(solution)/shard_map/psum | solution.py:108
  1900.2 0.7 copy.47
  1900.9 1.5 add.106
  1902.4 0.3 convolution_bitcast_fusion.2
  1902.7 0.2 convolution_multiply_fusion.1
  1902.9 1.9 reduce.13
  1904.8 0.3 reshape.268
  1905.1 11.5 scatter_fusion
  1916.8 0.9 convolution_bitcast_fusion
  1917.8 1.1 fusion.15
  1918.9 330.9 %all-reduce.4.cloned.1.call-done = (f32[256,128]{0,1:T(8,128)}, f32[256,128]{1,0:T(8,128)}, f32[128,256]{1,0:T(8,128)}) async-done(((f32[256,128]{0,1:T(8,128)}, f32[256,128]{1,0:T(8,128)}, f32[128,256]{1,0:T(8,128)}), (f32[256,128]{0,1:T(8,128)}, f32[256,128]{1,0:T(8,128)}, f32[128,256]{1,0:T(8,128)})) %all-reduce.4.cloned.1.call-update) | async-done | bytes 393232 | tf_op jit(solution)/shard_map/psum | solution.py:108
  2249.9 1.5 slice_multiply_fusion
  2251.4 1.6 broadcast_multiply_fusion.1
  2253.0 1.6 broadcast_multiply_fusion
  2254.6 21.7 reduce-scatter.8.cloned.1.call-done
  2276.3 1.7 fusion.3
  (105 shorter events, 1.7 us)
Async XLA Ops:
  7.2 814.8 %copy-start = (f32[256,256]{1,0:T(8,128)S(1)}, f32[256,256]{1,0:T(8,128)}, u32[]{:S(2)}) copy-start(f32[256,256]{1,0:T(8,128)} %param.19) | copy-start | bytes 786436
  11.2 292.6 %copy-start.7 = (f32[256,128]{0,1:T(8,128)}, f32[256,128]{0,1:T(8,128)S(1)}, u32[]{:S(2)}) copy-start(f32[256,128]{0,1:T(8,128)S(1)} %convolution_bitcast_fusion.1) | copy-start | bytes 393220
  16.8 21.9 copy-start.29
  16.8 22.5 copy-start.11
  16.8 22.6 copy-start.22
  16.8 22.8 copy-start.2
  18.2 773.0 %all-to-all-start = ((f32[128,1,1024]{2,1,0:T(1,128)}), f32[128,1,1024]{2,1,0:T(1,128)S(1)}, u32[]{:S(2)}, u32[]{:S(2)}) async-start(f32[128,1,1024]{2,1,0:T(1,128)} %reshape.265), calls=%async_computation | async-start | bytes 1048576 | tf_op jit(solution)/shard_map/all_to_all | solution.py:40
  38.6 819.0 %reduce-scatter.6.cloned.1.call-start = ((), (), s32[]{:S(2)}) async-start(), calls=%async_computation.6 | async-start | bytes 327680 | tf_op jit(solution)/shard_map/reduce_scatter | solution.py:72
  40.8 753.3 %copy-start.3 = (f32[256,64]{0,1:T(8,128)}, f32[256,64]{0,1:T(8,128)S(1)}, u32[]{:S(2)}) copy-start(f32[256,64]{0,1:T(8,128)S(1)} %get-tuple-element.38) | copy-start | bytes 196612
  303.6 0.6 copy-start.31
  790.1 1.0 copy-start.33
  790.1 3.9 copy-start.18
  790.2 21.0 copy-start.16
  790.5 3.6 copy-start.24
  790.5 20.7 copy-start.5
  808.3 2.9 copy-start.21
  808.3 2.9 copy-start.25
  808.3 2.9 copy-start.27
  808.3 2.9 copy-start.30
  808.3 13.0 copy-start.9
  808.3 13.6 copy-start.35
  811.1 12.5 copy-start.23
  811.4 9.9 copy-start.13
  822.0 39.0 %copy-start.20 = (f32[256,128]{1,0:T(8,128)}, f32[256,128]{1,0:T(8,128)S(1)}, u32[]{:S(2)}) copy-start(f32[256,128]{1,0:T(8,128)S(1)} %fusion.49) | copy-start | bytes 393220
  822.3 38.6 %copy-start.10 = (f32[256,128]{1,0:T(8,128)}, f32[256,128]{1,0:T(8,128)S(1)}, u32[]{:S(2)}) copy-start(f32[256,128]{1,0:T(8,128)S(1)} %convolution_multiply_fusion) | copy-start | bytes 393220
  823.5 1077.4 %reduce-scatter.4.cloned.1.call-start = ((), (), s32[]{:S(2)}) async-start(), calls=%async_computation.5 | async-start | bytes 327680 | tf_op jit(solution)/shard_map/reduce_scatter | solution.py:68
  884.1 524.9 %copy-start.1 = (f32[2304,64]{1,0:T(8,128)}, f32[2304,64]{1,0:T(8,128)S(1)}, u32[]{:S(2)}) copy-start(f32[2304,64]{1,0:T(8,128)S(1)} %scatter_custom_fusion) | copy-start | bytes 1769476
  884.1 24.5 %copy-start.6 = (f32[64,256]{1,0:T(8,128)S(1)}, f32[64,256]{1,0:T(8,128)}, u32[]{:S(2)}) copy-start(f32[64,256]{1,0:T(8,128)} %copy-done.5) | copy-start | bytes 196612
  884.2 24.5 %copy-start.26 = (f32[256]{0:T(256)S(1)}, f32[256]{0:T(256)}, u32[]{:S(2)}) copy-start(f32[256]{0:T(256)} %copy-done.24) | copy-start | bytes 3076
  884.2 24.5 %copy-start.28 = (f32[256]{0:T(256)S(1)}, f32[256]{0:T(256)}, u32[]{:S(2)}) copy-start(f32[256]{0:T(256)} %fusion.28) | copy-start | bytes 3076
  884.2 524.5 %copy-start.4 = (f32[256,64]{0,1:T(8,128)S(1)}, f32[256,64]{0,1:T(8,128)}, u32[]{:S(2)}) copy-start(f32[256,64]{0,1:T(8,128)} %copy-done.3) | copy-start | bytes 196612
  884.2 524.4 %copy-start.8 = (f32[256,128]{0,1:T(8,128)S(1)}, f32[256,128]{0,1:T(8,128)}, u32[]{:S(2)}) copy-start(f32[256,128]{0,1:T(8,128)} %copy-done.7) | copy-start | bytes 393220
  885.7 23.0 %copy-start.15 = (f32[256,64]{0,1:T(8,128)S(1)}, f32[256,64]{0,1:T(8,128)}, u32[]{:S(2)}) copy-start(f32[256,64]{0,1:T(8,128)} %get-tuple-element.34) | copy-start | bytes 196612
  885.7 23.0 %copy-start.17 = (f32[64,64]{0,1:T(8,128)S(1)}, f32[64,64]{0,1:T(8,128)}, u32[]{:S(2)}) copy-start(f32[64,64]{0,1:T(8,128)} %copy-done.16) | copy-start | bytes 49156
  885.7 522.9 %copy-start.19 = (f32[64,1,64]{0,2,1:T(8,128)S(1)}, f32[64,1,64]{0,2,1:T(8,128)}, u32[]{:S(2)}) copy-start(f32[64,1,64]{0,2,1:T(8,128)} %copy-done.18) | copy-start | bytes 49156
  885.7 522.9 %copy-start.34 = (f32[64]{0:T(128)S(1)}, f32[64]{0:T(128)}, u32[]{:S(2)}) copy-start(f32[64]{0:T(128)} %copy-done.33) | copy-start | bytes 772
  885.7 523.0 %copy-start.32 = (f32[64]{0:T(128)S(1)}, f32[64]{0:T(128)}, u32[]{:S(2)}) copy-start(f32[64]{0:T(128)} %copy-done.31) | copy-start | bytes 772
  885.7 1015.2 %copy-start.14 = (f32[256,64]{0,1:T(8,128)S(1)}, f32[256,64]{0,1:T(8,128)}, u32[]{:S(2)}) copy-start(f32[256,64]{0,1:T(8,128)} %copy-done.13) | copy-start | bytes 196612
  885.7 1017.2 %all-to-all-start.1 = ((f32[128,1,1024]{2,1,0:T(1,128)}), f32[128,1,1024]{2,1,0:T(1,128)S(1)}, u32[]{:S(2)}, u32[]{:S(2)}) async-start(f32[128,1,1024]{2,1,0:T(1,128)} %reshape.267), calls=%async_computation.3 | async-start | bytes 1048576 | tf_op jit(solution)/shard_map/all_to_all | solution.py:94
  904.7 1345.2 %all-reduce.4.cloned.1.call-start = ((), (), s32[]{:S(2)}) async-start(), calls=%async_computation.8 | async-start | bytes 786432 | tf_op jit(solution)/shard_map/psum | solution.py:108
  1408.9 496.2 %slice-start = ((f32[2304,64]{1,0:T(8,128)}), f32[256,64]{1,0:T(8,128)S(1)}, s32[]{:S(2)}) async-start(f32[2304,64]{1,0:T(8,128)} %copy-done.1), calls=%async_computation.9 | async-start | bytes 262144 | tf_op jit(solution)/shard_map/slice | solution.py:101
  1916.7 359.6 %copy-start.12 = (f32[64,64]{1,0:T(8,128)S(1)}, f32[64,64]{1,0:T(8,128)}, u32[]{:S(2)}) copy-start(f32[64,64]{1,0:T(8,128)} %param.11) | copy-start | bytes 49156
  1917.7 358.6 %reduce-scatter.8.cloned.1.call-start = ((), (), s32[]{:S(2)}) async-start(), calls=%async_computation.7 | async-start | bytes 327680 | tf_op jit(solution)/shard_map/reduce_scatter | solution.py:105
Sparse Core Ops, SparseCore 0:
  823.6 33.9 reduce-scatter.5
  860.7 28.1 reduce-scatter.3
  1917.9 331.9 all-reduce.3
  2252.8 23.4 reduce-scatter.7
where the time goes:
time: 2290 us; the launch traced here: 2280 us
  blocking collectives  1750 us (76%)
  waiting for transfers between devices  385 us (17%)
  other arithmetic  52.9 us (2%)
  starting transfers between devices  39.5 us (2%)
  local copies, waits for them, and re-layouts  28.9 us (1%)
    psum x1, blocking collectives, on_device(): dfresh = lax.psum(dfresh_part, 'graph')  499 us
    psum x1, blocking collectives, on_device(): summed = lax.psum((grad_joined, grad_up, grad_down, dlatent_part), 'graph')  491 us
    psum x1, blocking collectives, on_device(): lax.psum((jnp.sum(weights, -1), einsum_exact('mha,ahe->mhe', weights, hea...  486 us
    psum x1, waiting for transfers between devices, on_device(): summed = lax.psum((grad_joined, grad_up, grad_down, dlatent_part), 'graph')  331 us
    pmax x1, blocking collectives, on_device(): global_top = lax.pmax(local_top, 'graph')  263 us
  transfers between devices with their start and end apart: 6, of which 3 were waited for; matrix products, arithmetic and copies ran while one was open for 2% of the time, Pallas kernels for 0%

commit v1 on v0

v1 whole, which is shorter than its diff:
```python
import functools
import math
from types import SimpleNamespace

import jax
import jax.numpy as jnp
from jax import lax
from jax.experimental import pallas as pl
from jax.experimental.pallas import tpu as pltpu
from jax.sharding import PartitionSpec as P

HEAD = 64
VN = 64
SLOTS = 16
LANES = 128
MESH = pl.DeviceIdType.MESH
F32 = jnp.float32
BF16 = jnp.bfloat16


def dot(left, right, contract, precision):
    return lax.dot_general(
        left, right, (contract, ((), ())), precision=precision, preferred_element_type=F32
    )


def mm(left, right):
    return dot(left, right, ((1,), (0,)), lax.Precision.HIGHEST)


def mt(left, right):
    return dot(left, right, ((1,), (1,)), lax.Precision.HIGHEST)


def mb(left, right):
    return dot(left, right, ((1,), (0,)), lax.Precision.DEFAULT)


def mbt(left, right):
    return dot(left, right, ((1,), (1,)), lax.Precision.DEFAULT)


def split(x, axis):
    high = x.astype(BF16)
    low = (x - high.astype(F32)).astype(BF16)
    return jnp.concatenate([high, low], axis)


def halves(x):
    half = x.shape[0] // 2
    return x[:half] + x[half:]


def layer(nz, nxc, nmp, rows, dim, names, *refs):
    r = SimpleNamespace(**dict(zip(names, refs)))
    graph = lax.axis_index("graph")
    mp = lax.axis_index("mp")
    z = graph // nxc
    xc = lax.rem(graph, nxc)
    nb4 = nz // 4
    zb = z // 4
    zm = lax.rem(z, 4)
    ng = nz * nxc
    scale = 1.0 / math.sqrt(HEAD)
    factor = 1.0 / math.sqrt(rows * ng)

    def z_peer(d):
        return lax.rem(z + d, nz)

    def x_peer(d):
        return lax.rem(xc + d, nxc)

    def send(src, dst, ssem, rsem, device):
        pltpu.make_async_remote_copy(
            src_ref=src,
            dst_ref=dst,
            send_sem=ssem,
            recv_sem=rsem,
            device_id=device,
            device_id_type=MESH,
        ).start()

    def wait(ref, sem):
        pltpu.make_async_copy(ref, ref, sem).wait()

    def loop(low, high, body):
        def step(d, carry):
            body(d)
            return carry

        lax.fori_loop(low, high, step, 0)

    barrier = pltpu.get_barrier_semaphore()

    def greet(device):
        pl.semaphore_signal(barrier, inc=1, device_id=device, device_id_type=MESH)

    loop(1, nz, lambda d: greet({"graph": z_peer(d) * nxc + xc}))
    loop(1, nxc, lambda d: greet({"graph": z * nxc + x_peer(d)}))
    loop(1, nmp, lambda d: greet({"mp": lax.rem(mp + d, nmp)}))

    def group_start(give, got, sems):
        def go(d):
            peer = x_peer(d)
            send(give.at[peer], got.at[xc], sems.at[0], sems.at[1], {"graph": z * nxc + peer})

        loop(1, nxc, go)
        got[xc] = give[xc]

    def z_share(piece, got, sems):
        def go(d):
            send(piece, got.at[z], sems.at[2], sems.at[3], {"graph": z_peer(d) * nxc + xc})

        loop(1, nz, go)
        got[z] = piece[...]

    def group_gather(full, sems):
        def go(d):
            send(full.at[xc], full.at[xc], sems.at[4], sems.at[5], {"graph": z * nxc + x_peer(d)})

        loop(1, nxc, go)

    def wait_x(ref, sem):
        wait(ref.at[pl.ds(0, nxc - 1)], sem)

    def wait_z(ref, sem):
        wait(ref.at[pl.ds(0, nz - 1)], sem)

    def total(ref):
        acc = ref[0]
        for i in range(1, ref.shape[0]):
            acc = acc + ref[i]
        return acc

    def merged(ref):
        count = ref.shape[0]
        parts = [ref[i] for i in range(count)]
        tops = [part[:, 96:97] for part in parts]
        top = functools.reduce(jnp.maximum, tops)
        acc = parts[0] * jnp.exp(tops[0] - top)
        for i in range(1, count):
            acc = acc + parts[i] * jnp.exp(tops[i] - top)
        lane = lax.broadcasted_iota(jnp.int32, acc.shape, 1)
        return jnp.where(lane >= 96, top, acc)

    def rows_start(out, mid, zs, zr):
        for i in (0, 1, 3, 2)[: nb4] if nb4 != 2 else (0, 1):
            base = lax.rem(zb + nb4 - i, nb4) * 4
            for d in range(1 if i == 0 else 0, 4):
                peer = base + lax.rem(zm + d, 4)
                send(out.at[peer], mid.at[z], zs, zr.at[i], {"graph": peer * nxc + xc})
        mid[z] = out[z]

    def rows_forward(i, mid, land, zr, fs, fr):
        base = lax.rem(zb + i, nb4) * 4
        wait(mid.at[pl.ds(0, 3 if i == 0 else 4)], zr.at[i])

        def go(d):
            peer = x_peer(d)
            send(
                mid.at[pl.ds(base, 4), peer],
                land.at[pl.ds(base, 4), xc],
                fs,
                fr,
                {"graph": z * nxc + peer},
            )

        loop(1, nxc, go)
        land[pl.ds(base, 4), xc] = mid[pl.ds(base, 4), xc]

    def rows_wait(land, fr):
        wait(land.at[:, pl.ds(0, nxc - 1)], fr)

    def y_send(src_of, got, ssem, rsem):
        for d in range(1, nmp):
            peer = lax.rem(mp + d, nmp)
            send(src_of(peer), got.at[mp], ssem, rsem, {"mp": peer})

    def wait_y(ref, sem):
        wait(ref.at[pl.ds(0, nmp - 1)], sem)

    xt_all = r.agents[...].T
    r.xt[...] = xt_all.reshape(nmp, HEAD, rows)
    w_joined = jnp.concatenate([r.w_local[...], r.w_value[...]], 1)
    joined_t = mm(w_joined.T, xt_all)
    lt2 = split(joined_t[:HEAD], 0)
    r.lt2[...] = lt2
    r.vt[:HEAD] = joined_t[HEAD:]
    r.vt[HEAD:] = jnp.ones((HEAD, rows), F32)
    half = ng * 8
    chunk = 256
    for c in range(2 * half // chunk):
        cols = pl.ds(c * chunk, chunk)
        row_id = lax.broadcasted_iota(jnp.int32, (rows, chunk), 0)
        r.st[:, cols] = jnp.where(row_id == r.sends[:, cols], 1.0, 0.0).astype(BF16)
    rows_out = halves(mb(lt2, r.st[...]))
    packed = jnp.concatenate([rows_out[:, :half], rows_out[:, half:]], 0).T
    r.out1[...] = packed.reshape(nz, nxc, 8, LANES)
    pl.semaphore_wait(barrier, nz + nxc + nmp - 3)
    rows_start(r.out1, r.mid1, r.rsem.at[0], r.zsem1)

    xt = r.xt[mp]
    scores = mm(r.latents[...], xt) * scale
    local_top = jnp.max(scores, 1, keepdims=True)
    weights = jnp.exp(scores - local_top)
    r.weights[...] = weights
    part = mt(weights, r.vt[...])
    lane = lax.broadcasted_iota(jnp.int32, part.shape, 1)
    r.give1[...] = jnp.where(lane >= 96, local_top, part).reshape(r.give1.shape)
    group_start(r.give1, r.got1, r.s1)

    degree = r.degree[...].astype(F32)
    degree_col = jnp.broadcast_to(degree, (8, rows)).T[:, :1]
    slot = lax.broadcasted_iota(jnp.int32, (rows, SLOTS), 1)
    near = r.neighbours[...]
    far = near - rows
    k = far & 15
    far_col = rows + (k >> 3) * half + (far >> 4) * 8 + (k & 7)
    column = jnp.where(near < rows, near, far_col)
    r.nbm[...] = jnp.where(slot.astype(F32) < degree_col, column, -1)
    width = rows + 2 * half
    part_width = 768 if width % 768 == 0 else 256

    def count_rows(b):
        row = pl.multiple_of(b * 16, 16)
        nb = r.nbm[pl.ds(row, 16), :]
        for c in range(width // part_width):
            col = lax.broadcasted_iota(jnp.int32, (16, part_width), 1) + c * part_width
            acc = jnp.zeros((16, part_width), F32)
            for s in range(SLOTS):
                acc = acc + jnp.where(nb[:, s : s + 1] == col, 1.0, 0.0)
            r.counts[pl.ds(row, 16), pl.ds(c * part_width, part_width)] = acc.astype(BF16)

    def count_part(p):
        blocks = rows // 64
        loop(p * blocks, (p + 1) * blocks, count_rows)

    ct_all = r.cotangent[...].T
    r.ct[...] = ct_all.reshape(nmp, HEAD, rows)
    r.dact[...] = mm(r.w_down[...], ct_all)
    r.wut[...] = r.w_up[...].T
    r.wdt[...] = r.w_down[...].T

    wait_x(r.got1, r.s1.at[1])
    r.piece1[...] = merged(r.got1)
    z_share(r.piece1, r.gotz1, r.s1)
    rows_forward(0, r.mid1, r.land1, r.zsem1, r.rsem.at[1], r.rsem.at[2])
    count_part(0)
    wait_z(r.gotz1, r.s1.at[3])
    r.full1[xc] = merged(r.gotz1)
    group_gather(r.full1, r.s1)
    order = {1: (), 2: (1,), 4: (1, 3, 2)}[nb4]
    for p, i in enumerate(order):
        rows_forward(i, r.mid1, r.land1, r.zsem1, r.rsem.at[1], r.rsem.at[2])
        count_part(p + 1)
    for p in range(len(order) + 1, 4):
        count_part(p)

    wait_x(r.full1, r.s1.at[5])
    soft = r.full1[...].reshape(VN, LANES)
    inv_total = 1.0 / soft[:, 64:65]
    attended = soft[:, :HEAD] * inv_total
    r.attended[...] = attended
    r.weights[...] = r.weights[...] * (jnp.exp(local_top - soft[:, 96:97]) * inv_total)
    fresh = r.latents[...] + attended
    r.fresh[...] = fresh
    a_scores = mm(fresh, xt) * scale
    a_exp = jnp.exp(a_scores - jnp.max(a_scores, 0, keepdims=True))
    a_prob = a_exp / jnp.sum(a_exp, 0, keepdims=True)
    r.aprob[...] = a_prob
    r.fresh_t[...] = fresh.T
    readout = mm(r.fresh_t[...], a_prob)
    own = mbt(r.lt2[...], r.counts[:, pl.ds(0, rows)])

    def packed_product(left_low, left_high, land):
        both = split(land[...].reshape(half, LANES), 1)
        low = mb(left_low, both)
        high = mb(left_high, both)
        lane2 = lax.broadcasted_iota(jnp.int32, low.shape, 1) % LANES
        picked = jnp.where(lane2 < HEAD, low, high)
        return (picked[:, :LANES] + picked[:, LANES:]).T

    rows_wait(r.land1, r.rsem.at[2])
    far_sum = packed_product(
        r.counts[:, pl.ds(rows, half)], r.counts[:, pl.ds(rows + half, half)], r.land1
    )
    inv_degree = 1.0 / degree
    message = halves(own + far_sum) * inv_degree
    hidden = xt + message + readout
    r.hid[mp] = hidden
    y_send(lambda peer: r.hid.at[mp], r.hid, r.ysem.at[0], r.ysem.at[1])
    wait_y(r.hid, r.ysem.at[1])

    hid_all = r.hid[...].reshape(dim, rows)
    pre = mm(r.wut[...], hid_all)
    gate = 1.0 / (1.0 + jnp.exp(-pre))
    dpre = r.dact[...] * (gate * (1.0 + pre * (1.0 - gate)))
    r.dhp[...] = mm(r.w_up[...], dpre).reshape(r.dhp.shape)
    y_send(lambda peer: r.dhp.at[peer], r.rdh, r.ysem.at[2], r.ysem.at[3])
    act = pre * gate
    r.brp[...] = mm(r.wdt[...], act).reshape(r.brp.shape)
    y_send(lambda peer: r.brp.at[peer], r.rbr, r.ysem.at[4], r.ysem.at[5])
    r.rdh[mp] = r.dhp[mp] + r.ct[mp]
    r.rbr[mp] = r.brp[mp] + hidden
    wait_y(r.rdh, r.ysem.at[3])
    dhid = total(r.rdh)
    r.dhid[...] = dhid

    dtable = halves(mb(split(dhid * inv_degree, 0), r.counts[...]))
    back = jnp.concatenate([dtable[:, rows : rows + half], dtable[:, rows + half :]], 0).T
    r.out2[...] = back.reshape(r.out2.shape)
    rows_start(r.out2, r.mid2, r.rsem.at[3], r.zsem2)
    r.down[...] = dtable[:, :rows]

    dprob = mm(r.fresh[...], dhid)
    a_prob = r.aprob[...]
    dagent = a_prob * (dprob - jnp.sum(a_prob * dprob, 0, keepdims=True)) * scale
    dfresh_part = mt(dagent, xt) + mt(a_prob, dhid)
    r.give2[...] = jnp.concatenate(
        [dfresh_part, jnp.zeros((VN, LANES - HEAD), F32)], 1
    ).reshape(r.give2.shape)
    group_start(r.give2, r.got2, r.s2)
    r.dx[...] = dhid + mm(r.fresh_t[...], dagent)
    units = r.w_up.shape[1]
    grad_up = mt(hid_all, dpre)
    grad_down = mt(act, ct_all)

    def put3(row, value):
        r.give3[pl.ds(row, value.shape[0]), :] = value

    put3(0, grad_up)
    blocks = dim // LANES
    for b in range(blocks):
        put3(dim + b * units, grad_down[:, b * LANES : (b + 1) * LANES])
    base_value = dim + blocks * units
    base_latent = base_value + blocks * HEAD
    pad3 = r.give3.shape[0] - base_latent - VN
    if pad3:
        put3(base_latent + VN, jnp.zeros((pad3, LANES), F32))
    wait_x(r.got2, r.s2.at[1])
    r.piece2[...] = total(r.got2)
    z_share(r.piece2, r.gotz2, r.s2)
    rows_forward(0, r.mid2, r.land2, r.zsem2, r.rsem.at[4], r.rsem.at[5])
    wait_z(r.gotz2, r.s2.at[3])
    r.full2[xc] = total(r.gotz2)
    group_gather(r.full2, r.s2)
    wait_y(r.rbr, r.ysem.at[5])
    r.updated[...] = total(r.rbr).T
    if len(order) > 0:
        rows_forward(order[0], r.mid2, r.land2, r.zsem2, r.rsem.at[4], r.rsem.at[5])
    wait_x(r.full2, r.s2.at[5])
    dfresh = r.full2[...].reshape(VN, LANES)[:, :HEAD]

    prob = r.weights[...]
    vt = r.vt[:HEAD]
    dvt = mm(dfresh.T, prob)
    dweights = mm(dfresh, vt)
    centre = jnp.sum(dfresh * r.attended[...], 1, keepdims=True)
    dscores = prob * (dweights - centre) * scale
    dlatent = mt(dscores, xt)
    xt_flat = r.xt[...].reshape(dim, rows)
    grad_value = mt(dvt, xt_flat)
    for b in range(blocks):
        put3(base_value + b * HEAD, grad_value[:, b * LANES : (b + 1) * LANES])
    put3(base_latent, jnp.concatenate([dlatent, jnp.zeros((VN, LANES - HEAD), F32)], 1))
    rows3 = r.give3.shape[0] // nxc
    tile3 = rows3 // nz

    def piece3(i):
        return pl.ds(pl.multiple_of(i * rows3, 8), rows3)

    def start3(d):
        peer = x_peer(d)
        send(
            r.give3.at[piece3(peer)], r.got3.at[xc], r.s3.at[0], r.s3.at[1],
            {"graph": z * nxc + peer},
        )

    loop(1, nxc, start3)
    r.got3[xc] = r.give3[piece3(xc), :]
    r.dx[...] = r.dx[...] + mm(r.latents[...].T, dscores)
    dthrough_value = mm(r.w_value[...], dvt)
    for i in order[1:]:
        rows_forward(i, r.mid2, r.land2, r.zsem2, r.rsem.at[4], r.rsem.at[5])
    wait_x(r.got3, r.s3.at[1])
    r.piece3[...] = total(r.got3).reshape(nz, tile3, LANES)

    def scatter3(d):
        peer = z_peer(d)
        send(
            r.piece3.at[peer], r.gotz3.at[z], r.s3.at[2], r.s3.at[3],
            {"graph": peer * nxc + xc},
        )

    loop(1, nz, scatter3)
    r.gotz3[z] = r.piece3[z]
    wait_z(r.gotz3, r.s3.at[3])
    r.full3[xc, z] = total(r.gotz3)

    def gather3(d):
        send(
            r.full3.at[xc, z], r.full3.at[xc, z], r.s3.at[4], r.s3.at[5],
            {"graph": z_peer(d) * nxc + xc},
        )

    loop(1, nz, gather3)

    rows_wait(r.land2, r.rsem.at[5])
    far_back = packed_product(r.st[:, pl.ds(0, half)], r.st[:, pl.ds(half, half)], r.land2)
    dlocal = r.down[...] + halves(far_back)
    grad_local = mt(dlocal, xt_flat)
    r.give4[...] = jnp.concatenate(
        [grad_local[:, b * LANES : (b + 1) * LANES] for b in range(blocks)], 0
    ).reshape(r.give4.shape)
    group_start(r.give4, r.got4, r.s4)
    r.dtp[...] = (mm(r.w_local[...], dlocal) + dthrough_value).reshape(r.dtp.shape)
    y_send(lambda peer: r.dtp.at[peer], r.rdt, r.ysem.at[6], r.ysem.at[7])
    r.rdt[mp] = r.dtp[mp] + r.dx[...]
    wait(r.full3.at[0, pl.ds(0, nz - 1)], r.s3.at[5])

    def spread3(d):
        send(
            r.full3.at[xc], r.full3.at[xc], r.s3.at[6], r.s3.at[7],
            {"graph": z * nxc + x_peer(d)},
        )

    loop(1, nxc, spread3)
    wait_x(r.got4, r.s4.at[1])
    r.piece4[...] = total(r.got4)
    z_share(r.piece4, r.gotz4, r.s4)
    wait_y(r.rdt, r.ysem.at[7])
    r.grad_agents[...] = total(r.rdt).T
    wait_x(r.full3, r.s3.at[7])
    sums = r.full3[...].reshape(r.give3.shape) * factor
    r.grad_up[...] = sums[:dim]
    for b in range(blocks):
        r.grad_down[:, b * LANES : (b + 1) * LANES] = sums[dim + b * units : dim + (b + 1) * units]
    for b in range(blocks):
        low = base_value + b * HEAD
        r.grad_value[b * LANES : (b + 1) * LANES, :] = sums[low : low + HEAD].T
    r.grad_latents[...] = dfresh * factor + sums[base_latent : base_latent + VN, :HEAD]
    wait_z(r.gotz4, r.s4.at[3])
    r.full4[xc] = total(r.gotz4)
    group_gather(r.full4, r.s4)

    for give, got_z, sems in (
        (r.give1, r.gotz1, r.s1),
        (r.give2, r.gotz2, r.s2),
        (r.give4, r.gotz4, r.s4),
    ):
        wait_x(give, sems.at[0])
        wait_z(got_z, sems.at[2])
    wait_x(r.full1, r.s1.at[4])
    wait_x(r.full2, r.s2.at[4])
    wait_x(r.got3, r.s3.at[0])
    wait_z(r.gotz3, r.s3.at[2])
    wait(r.full3.at[0, pl.ds(0, nz - 1)], r.s3.at[4])
    wait_x(r.full3, r.s3.at[6])
    for mid, land, base in ((r.mid1, r.land1, 0), (r.mid2, r.land2, 3)):
        wait(mid.at[pl.ds(0, nz - 1)], r.rsem.at[base])
        wait(land.at[:, pl.ds(0, nxc - 1)], r.rsem.at[base + 1])
    for ref, i in ((r.hid, 0), (r.rdh, 2), (r.rbr, 4), (r.rdt, 6)):
        wait_y(ref, r.ysem.at[i])
    wait_x(r.full4, r.s4.at[5])
    final = r.full4[...].reshape(blocks * HEAD, LANES) * factor
    for b in range(blocks):
        r.grad_local[b * LANES : (b + 1) * LANES, :] = final[b * HEAD : (b + 1) * HEAD].T
    wait_x(r.full4, r.s4.at[4])


def on_device(
    nz, agents, latents, w_local, w_value, w_up, w_down, neighbours, degree, send_rows, cotangent
):
    rows, dim = agents.shape
    ng = lax.axis_size("graph")
    nmp = lax.axis_size("mp")
    nxc = ng // nz
    units = w_up.shape[1]
    sends = send_rows[0].reshape(ng, 2, 8).transpose(1, 0, 2).reshape(1, ng * SLOTS)
    inputs = dict(
        agents=agents,
        latents=latents,
        w_local=w_local,
        w_value=w_value,
        w_up=w_up,
        w_down=w_down,
        neighbours=neighbours,
        degree=degree.reshape(1, rows),
        sends=sends,
        cotangent=cotangent,
    )
    outs = dict(
        updated=(rows, HEAD),
        grad_agents=(rows, HEAD),
        grad_latents=(VN, HEAD),
        grad_local=(dim, HEAD),
        grad_value=(dim, HEAD),
        grad_up=(dim, units),
        grad_down=(units, dim),
    )
    half = ng * 8
    blocks = dim // LANES
    step = 8 * nz
    need = (dim + blocks * units + blocks * HEAD + VN) // nxc
    rows3 = -(-need // step) * step
    rows4 = blocks * HEAD // nxc
    rows1 = VN // nxc
    vmem = lambda *shape: pltpu.VMEM(shape, F32)
    dma = lambda n: pltpu.SemaphoreType.DMA((n,))
    scratch = dict(
        xt=vmem(nmp, HEAD, rows),
        lt2=pltpu.VMEM((2 * HEAD, rows), BF16),
        vt=vmem(2 * HEAD, rows),
        st=pltpu.VMEM((rows, 2 * half), BF16),
        counts=pltpu.VMEM((rows, rows + 2 * half), BF16),
        nbm=pltpu.VMEM((rows, SLOTS), jnp.int32),
        weights=vmem(VN, rows),
        aprob=vmem(VN, rows),
        attended=vmem(VN, HEAD),
        fresh=vmem(VN, HEAD),
        fresh_t=vmem(HEAD, VN),
        ct=vmem(nmp, HEAD, rows),
        dact=vmem(units, rows),
        wut=vmem(units, dim),
        wdt=vmem(dim, units),
        hid=vmem(nmp, HEAD, rows),
        dhp=vmem(nmp, HEAD, rows),
        rdh=vmem(nmp, HEAD, rows),
        brp=vmem(nmp, HEAD, rows),
        rbr=vmem(nmp, HEAD, rows),
        dtp=vmem(nmp, HEAD, rows),
        rdt=vmem(nmp, HEAD, rows),
        dhid=vmem(HEAD, rows),
        down=vmem(HEAD, rows),
        dx=vmem(HEAD, rows),
        give3=vmem(nxc * rows3, LANES),
        got3=vmem(nxc, rows3, LANES),
        piece3=vmem(nz, rows3 // nz, LANES),
        gotz3=vmem(nz, rows3 // nz, LANES),
        full3=vmem(nxc, nz, rows3 // nz, LANES),
        s3=dma(8),
        rsem=dma(6),
        zsem1=dma(4),
        zsem2=dma(4),
        ysem=dma(8),
    )
    for i in (1, 2):
        scratch["out%d" % i] = vmem(nz, nxc, 8, LANES)
        scratch["mid%d" % i] = vmem(nz, nxc, 8, LANES)
        scratch["land%d" % i] = vmem(nz, nxc, 8, LANES)
    for i, n in ((1, rows1), (2, rows1), (4, rows4)):
        scratch["give%d" % i] = vmem(nxc, n, LANES)
        scratch["got%d" % i] = vmem(nxc, n, LANES)
        scratch["piece%d" % i] = vmem(n, LANES)
        scratch["gotz%d" % i] = vmem(nz, n, LANES)
        scratch["full%d" % i] = vmem(nxc, n, LANES)
        scratch["s%d" % i] = dma(6)
    names = list(inputs) + list(outs) + list(scratch)
    spec = pl.BlockSpec(memory_space=pltpu.VMEM)
    result = pl.pallas_call(
        functools.partial(layer, nz, nxc, nmp, rows, dim, names),
        out_shape=[jax.ShapeDtypeStruct(shape, F32) for shape in outs.values()],
        in_specs=[spec] * len(inputs),
        out_specs=[spec] * len(outs),
        scratch_shapes=list(scratch.values()),
        compiler_params=pltpu.CompilerParams(
            collective_id=0, has_side_effects=True, vmem_limit_bytes=40 * 1024 * 1024
        ),
        name="layer",
    )(*inputs.values())
    return tuple(result)


def solution(mesh, nz=16):
    return jax.shard_map(
        functools.partial(on_device, nz),
        mesh=mesh,
        in_specs=(
            P("graph", None),
            P(None, "mp"),
            P(None, "mp"),
            P(None, "mp"),
            P(None, "mp"),
            P("mp", None),
            P("graph", None),
            P("graph"),
            P("graph", None, None),
            P("graph", None),
        ),
        out_specs=(
            P("graph", "mp"),
            P("graph", "mp"),
            P(None, "mp"),
            P(None, "mp"),
            P(None, "mp"),
            P(None, "mp"),
            P("mp", None),
        ),
        check_vma=False,
    )
```

time: 2290 us -> 148 us (0.06)
  blocking collectives: 1750 us -> 0 us
  waiting for transfers between devices: 385 us -> 0 us
  Pallas kernels: 0 us -> 138 us
  other arithmetic: 52.9 us -> 0 us
  starting transfers between devices: 39.5 us -> 0 us
    psum x3 -> x0, blocking collectives: 1480 us -> none  [the longest x1 499 us: on_device(): dfresh = lax.psum(dfresh_part, 'graph')]
    psum x1 -> x0, waiting for transfers between devices: 331 us -> none  [on_device(): summed = lax.psum((grad_joined, grad_up, grad_down, dlatent_part), 'graph')]
    pmax x1 -> x0, blocking collectives: 263 us -> none  [on_device(): global_top = lax.pmax(local_top, 'graph')]
    pallas_call x0 -> x1, Pallas kernels: none -> 138 us  [on_device(): pl.pallas_call(functools.partial(layer, nz, nxc, nmp, rows, dim, names),...]
    reduce_scatter x3 -> x0, waiting for transfers between devices: 54 us -> none  [the longest x1 32.3 us: on_device(): lax.psum_scatter(matmul(dpre_act, w_up.T), 'mp', scatter_dimension=1, til...]
    all_to_all x2 -> x0, starting transfers between devices: 39.4 us -> none  [the longest x1 20.4 us: on_device(): lax.all_to_all(outgoing, 'graph', split_axis=0, concat_axis=0, tiled=True)]
    scatter-add x2 -> x0, other arithmetic: 34.7 us -> none  [the longest x1 23.1 us: on_device(): jax.ops.segment_sum(spread_grad.reshape(-1, col_count), neighbours.reshap...]
  transfers between devices with their start and end apart: 6 -> 0, of which waited for: 3 -> 0; matrix products, arithmetic and copies ran while one was open for 2% -> 0% of each run, Pallas kernels for 0% -> 0%
where the time goes in v1:
time: 148 us
  Pallas kernels  138 us (93%)
  local copies, waits for them, and re-layouts  9.13 us (6%)
    pallas_call x1, Pallas kernels, on_device(): pl.pallas_call(functools.partial(layer, nz, nxc, nmp, rows, dim, names),...  138 us
    unnamed x18, local copies, waits for them, and re-layouts  5.34 us

profile of v1, /device:TPU:1, one launch (start us, length us, event | category | flops | bytes accessed | tf_op | source)
XLA Modules:
  0.0 147.9 jit_solution(106301205050318535)
XLA Ops:
  0.6 0.0 copy-start.2
  0.6 0.0 copy-start.3
  0.7 1.0 copy.26.refs_2_
  1.6 0.0 copy-start.1
  1.6 1.0 copy.27.refs_3_
  2.6 0.0 copy-start
  2.6 0.9 copy.28.refs_6_
  3.5 0.8 copy.25
  4.3 0.0 copy-start.4
  4.3 0.0 copy-start.5
  4.3 0.1 reshape.21.refs_8_
  4.5 0.0 copy-done.2
  4.5 0.0 copy-done.3
  4.5 0.0 copy-done.1
  4.5 0.0 copy-done
  4.5 0.6 copy-done.4
  5.1 0.0 copy-done.5
  5.1 138.0 %layer.1 = (f32[256,64]{1,0:T(8,128)S(1)}, f32[256,64]{1,0:T(8,128)S(1)}, f32[64,64]{1,0:T(8,128)S(1)}, f32[256,64]{1,0:T(8,128)S(1)}, f32[256,64]{1,0:T(8,128)S...) custom-call(f32[256,256]{1,0:T(8,128)S(1)} %copy-done, f32[64,64]{1,0:T(8,128)S(1)} %copy-done.4, ...), custom_call_target="tpu_custom_call" | custom-call | tf_op jit(solution)/shard_map/layer/pallas_call | solution.py:560
  143.1 0.7 copy.29
  143.8 0.7 copy.30
  144.5 0.7 copy.31
  145.3 0.7 copy.32
  146.0 0.6 copy.36
  146.6 0.7 copy.37
  147.2 0.7 copy.38
Async XLA Ops:
  0.6 3.8 %copy-start.2 = (f32[256,128]{1,0:T(8,128)S(1)}, f32[256,128]{1,0:T(8,128)}, u32[]{:S(2)}) copy-start(f32[256,128]{1,0:T(8,128)} %refs_4_.1) | copy-start | bytes 393220
  0.6 3.8 %copy-start.3 = (f32[128,256]{1,0:T(8,128)S(1)}, f32[128,256]{1,0:T(8,128)}, u32[]{:S(2)}) copy-start(f32[128,256]{1,0:T(8,128)} %refs_5_.1) | copy-start | bytes 393220
  1.6 2.9 %copy-start.1 = (f32[256,256]{1,0:T(8,128)S(1)}, f32[256,256]{1,0:T(8,128)}, u32[]{:S(2)}) copy-start(f32[256,256]{1,0:T(8,128)} %refs_9_.1) | copy-start | bytes 786436
  2.6 1.9 %copy-start = (f32[256,256]{1,0:T(8,128)S(1)}, f32[256,256]{1,0:T(8,128)}, u32[]{:S(2)}) copy-start(f32[256,256]{1,0:T(8,128)} %refs_0_.1) | copy-start | bytes 786436
  4.3 0.8 copy-start.4
  4.3 0.8 copy-start.5

commit v2 on v1

v2 whole, which is shorter than its diff:
```python
import functools
import math
from types import SimpleNamespace

import jax
import jax.numpy as jnp
from jax import lax
from jax.experimental import pallas as pl
from jax.experimental.pallas import tpu as pltpu
from jax.sharding import PartitionSpec as P

HEAD = 64
VN = 64
SLOTS = 16
LANES = 128
MESH = pl.DeviceIdType.MESH
F32 = jnp.float32
BF16 = jnp.bfloat16


def dot(left, right, contract, precision):
    return lax.dot_general(
        left, right, (contract, ((), ())), precision=precision, preferred_element_type=F32
    )


def mm(left, right):
    return dot(left, right, ((1,), (0,)), lax.Precision.HIGHEST)


def mt(left, right):
    return dot(left, right, ((1,), (1,)), lax.Precision.HIGHEST)


def mb(left, right):
    return dot(left, right, ((1,), (0,)), lax.Precision.DEFAULT)


def mbt(left, right):
    return dot(left, right, ((1,), (1,)), lax.Precision.DEFAULT)


def split(x, axis):
    high = x.astype(BF16)
    low = (x - high.astype(F32)).astype(BF16)
    return jnp.concatenate([high, low], axis)


def halves(x):
    half = x.shape[0] // 2
    return x[:half] + x[half:]


def layer(nz, nxc, nmp, rows, dim, names, given, *refs):
    r = SimpleNamespace(**dict(zip(names, refs)))
    loads = {
        name: pltpu.make_async_copy(getattr(r, name + "_hbm"), getattr(r, name), r.lsem.at[i])
        for i, name in enumerate(given)
    }
    for load in loads.values():
        load.start()
    graph = lax.axis_index("graph")
    mp = lax.axis_index("mp")
    z = graph // nxc
    xc = lax.rem(graph, nxc)
    nb4 = nz // 4
    zb = z // 4
    zm = lax.rem(z, 4)
    ng = nz * nxc
    scale = 1.0 / math.sqrt(HEAD)
    factor = 1.0 / math.sqrt(rows * ng)

    def z_peer(d):
        return lax.rem(z + d, nz)

    def x_peer(d):
        return lax.rem(xc + d, nxc)

    def send(src, dst, ssem, rsem, device):
        pltpu.make_async_remote_copy(
            src_ref=src,
            dst_ref=dst,
            send_sem=ssem,
            recv_sem=rsem,
            device_id=device,
            device_id_type=MESH,
        ).start()

    def wait(ref, sem):
        pltpu.make_async_copy(ref, ref, sem).wait()

    def loop(low, high, body):
        def step(d, carry):
            body(d)
            return carry

        lax.fori_loop(low, high, step, 0)

    barrier = pltpu.get_barrier_semaphore()

    def greet(device):
        pl.semaphore_signal(barrier, inc=1, device_id=device, device_id_type=MESH)

    loop(1, nz, lambda d: greet({"graph": z_peer(d) * nxc + xc}))
    loop(1, nxc, lambda d: greet({"graph": z * nxc + x_peer(d)}))
    loop(1, nmp, lambda d: greet({"mp": lax.rem(mp + d, nmp)}))

    def group_start(give, got, sems):
        def go(d):
            peer = x_peer(d)
            send(give.at[peer], got.at[xc], sems.at[0], sems.at[1], {"graph": z * nxc + peer})

        loop(1, nxc, go)
        got[xc] = give[xc]

    def z_share(piece, got, sems):
        def go(d):
            send(piece, got.at[z], sems.at[2], sems.at[3], {"graph": z_peer(d) * nxc + xc})

        loop(1, nz, go)
        got[z] = piece[...]

    def group_gather(full, sems):
        def go(d):
            send(full.at[xc], full.at[xc], sems.at[4], sems.at[5], {"graph": z * nxc + x_peer(d)})

        loop(1, nxc, go)

    def wait_x(ref, sem):
        wait(ref.at[pl.ds(0, nxc - 1)], sem)

    def wait_z(ref, sem):
        wait(ref.at[pl.ds(0, nz - 1)], sem)

    def total(ref):
        acc = ref[0]
        for i in range(1, ref.shape[0]):
            acc = acc + ref[i]
        return acc

    def merged(ref):
        count = ref.shape[0]
        parts = [ref[i] for i in range(count)]
        tops = [part[:, 96:97] for part in parts]
        top = functools.reduce(jnp.maximum, tops)
        acc = parts[0] * jnp.exp(tops[0] - top)
        for i in range(1, count):
            acc = acc + parts[i] * jnp.exp(tops[i] - top)
        lane = lax.broadcasted_iota(jnp.int32, acc.shape, 1)
        return jnp.where(lane >= 96, top, acc)

    def rows_x(i, out, mid, xs, xr):
        base = lax.rem(zb + nb4 - i, nb4) * 4

        def go(d):
            peer = x_peer(d)
            send(
                out.at[pl.ds(base, 4), peer],
                mid.at[pl.ds(base, 4), xc],
                xs,
                xr.at[i],
                {"graph": z * nxc + peer},
            )

        loop(1, nxc, go)
        mid[pl.ds(base, 4), xc] = out[pl.ds(base, 4), xc]

    def rows_z(i, mid, land, xr, zs, zr):
        base = lax.rem(zb + nb4 - i, nb4) * 4
        wait(mid.at[pl.ds(0, 4), pl.ds(0, nxc - 1)], xr.at[i])
        for d in range(1 if i == 0 else 0, 4):
            peer = base + lax.rem(zm + d, 4)
            send(mid.at[peer], land.at[z], zs, zr, {"graph": peer * nxc + xc})
        if i == 0:
            land[z] = mid[z]

    def rows_wait(land, zr):
        wait(land.at[pl.ds(0, nz - 1)], zr)

    def y_send(src_of, got, ssem, rsem):
        for d in range(1, nmp):
            peer = lax.rem(mp + d, nmp)
            send(src_of(peer), got.at[mp], ssem, rsem, {"mp": peer})

    def wait_y(ref, sem):
        wait(ref.at[pl.ds(0, nmp - 1)], sem)

    order = {1: (0,), 2: (1, 0), 4: (2, 1, 3, 0)}[nb4]
    rows1 = (r.mid1, r.land1, r.xsem1, r.rsem.at[1], r.rsem.at[2])
    rows2 = (r.mid2, r.land2, r.xsem2, r.rsem.at[4], r.rsem.at[5])

    half = ng * 8
    loads["agents"].wait()
    xt_all = r.agents[...].T
    r.xt[...] = xt_all.reshape(nmp, HEAD, rows)
    xt = r.xt[mp]
    xt2 = split(xt, 0)
    r.xt2[...] = xt2
    spread = lax.broadcasted_iota(jnp.int32, (ng, half), 1) // 8 == lax.broadcasted_iota(
        jnp.int32, (ng, half), 0
    )
    spread = jnp.where(spread, 1.0, 0.0).astype(BF16)
    loads["sends"].wait()
    wide = mb(r.sends[...].astype(F32).astype(BF16), spread)
    own_slot = lax.broadcasted_iota(jnp.int32, (8, half), 1) % 8 == lax.broadcasted_iota(
        jnp.int32, (8, half), 0
    )
    chunk = 256
    for h in range(2):
        line = jnp.sum(jnp.where(own_slot, wide[h * 8 : h * 8 + 8], 0.0), 0, keepdims=True)
        line = line.astype(jnp.int32)
        for c in range(half // chunk):
            row_id = lax.broadcasted_iota(jnp.int32, (rows, chunk), 0)
            hit = row_id == line[:, c * chunk : (c + 1) * chunk]
            r.st[:, pl.ds(h * half + c * chunk, chunk)] = jnp.where(hit, 1.0, 0.0).astype(BF16)
    rows_out = halves(mb(xt2, r.st[...]))
    packed = jnp.concatenate([rows_out[:, :half], rows_out[:, half:]], 0).T
    r.out1[...] = packed.reshape(nz, nxc, 8, LANES)

    loads["w_value_t"].wait()
    r.vt[:HEAD] = mm(r.w_value_t[...], xt_all)
    r.vt[HEAD:] = jnp.ones((HEAD, rows), F32)
    loads["latents"].wait()
    scores = mm(r.latents[...], xt) * scale
    local_top = jnp.max(scores, 1, keepdims=True)
    weights = jnp.exp(scores - local_top)
    r.weights[...] = weights
    part = mt(weights, r.vt[...])
    lane = lax.broadcasted_iota(jnp.int32, part.shape, 1)
    r.give1[...] = jnp.where(lane >= 96, local_top, part).reshape(r.give1.shape)
    pl.semaphore_wait(barrier, nz + nxc + nmp - 3)
    group_start(r.give1, r.got1, r.s1)
    for i in order:
        rows_x(i, r.out1, r.mid1, r.rsem.at[0], r.xsem1)

    loads["degree"].wait()
    loads["neighbours_t"].wait()
    degree = r.degree[...].astype(F32)
    inv_degree = 1.0 / degree
    slot = lax.broadcasted_iota(jnp.int32, (SLOTS, rows), 0)
    near = r.neighbours_t[...]
    far = near - rows
    k = far & 15
    far_col = rows + (k >> 3) * half + (far >> 4) * 8 + (k & 7)
    column = jnp.where(near < rows, near, far_col)
    column = jnp.where(slot < r.degree[...], column, -1)
    r.nbm[...] = column.astype(F32).T.astype(jnp.int32)
    width = rows + 2 * half
    part_width = 768 if width % 768 == 0 else 256

    def count_rows(b):
        row = pl.multiple_of(b * 16, 16)
        nb = r.nbm[pl.ds(row, 16), :]
        for c in range(width // part_width):
            col = lax.broadcasted_iota(jnp.int32, (16, part_width), 1) + c * part_width
            acc = jnp.zeros((16, part_width), F32)
            for s in range(SLOTS):
                acc = acc + jnp.where(nb[:, s : s + 1] == col, 1.0, 0.0)
            r.counts[pl.ds(row, 16), pl.ds(c * part_width, part_width)] = acc.astype(BF16)

    def count_part(p):
        blocks = rows // 64
        loop(p * blocks, (p + 1) * blocks, count_rows)

    wait_x(r.got1, r.s1.at[1])
    r.piece1[...] = merged(r.got1)
    z_share(r.piece1, r.gotz1, r.s1)
    for i in order:
        rows_z(i, *rows1)
    count_part(0)
    loads["w_local_t"].wait()
    r.wlt[mp] = r.w_local_t[...]
    y_send(lambda peer: r.w_local_t, r.wlt, r.ysem.at[0], r.ysem.at[1])
    count_part(1)
    count_part(2)
    loads["cotangent"].wait()
    loads["w_down"].wait()
    loads["w_up"].wait()
    ct_all = r.cotangent[...].T
    r.ct[...] = ct_all.reshape(nmp, HEAD, rows)
    r.dact[...] = mm(r.w_down[...], ct_all)
    r.wut[...] = r.w_up[...].T
    r.wdt[...] = r.w_down[...].T
    wait_z(r.gotz1, r.s1.at[3])
    r.full1[xc] = merged(r.gotz1)
    group_gather(r.full1, r.s1)
    count_part(3)
    wait_y(r.wlt, r.ysem.at[1])
    wl_t = r.wlt[...].reshape(dim, dim)
    wl = wl_t.T
    r.wl[...] = wl.reshape(nmp, HEAD, dim)
    r.wlu[...] = mm(wl, r.w_up[...])
    r.dmean_ct[...] = mm(r.wl[mp], ct_all)
    own = mbt(xt2, r.counts[:, pl.ds(0, rows)])

    wait_x(r.full1, r.s1.at[5])
    soft = r.full1[...].reshape(VN, LANES)
    inv_total = 1.0 / soft[:, 64:65]
    attended = soft[:, :HEAD] * inv_total
    prob = weights * (jnp.exp(local_top - soft[:, 96:97]) * inv_total)
    r.prob[...] = prob
    r.attended[...] = attended
    fresh = r.latents[...] + attended
    r.fresh[...] = fresh
    a_scores = mm(fresh, xt) * scale
    a_exp = jnp.exp(a_scores - jnp.max(a_scores, 0, keepdims=True))
    a_prob = a_exp / jnp.sum(a_exp, 0, keepdims=True)
    r.aprob[...] = a_prob
    r.fresh_t[...] = fresh.T
    r.read[mp] = mm(r.fresh_t[...], a_prob)
    y_send(lambda peer: r.read.at[mp], r.read, r.ysem.at[2], r.ysem.at[3])

    def put3(row, value):
        r.give3[pl.ds(row, value.shape[0]), :] = value

    blocks = dim // LANES
    units = r.w_up.shape[1]
    base_local = dim + blocks * units
    base_prob = base_local + blocks * HEAD
    end3 = base_prob + blocks * VN
    weighted_x = mt(prob, xt_all)
    for b in range(blocks):
        put3(base_prob + b * VN, weighted_x[:, b * LANES : (b + 1) * LANES])
    if r.give3.shape[0] > end3:
        put3(end3, jnp.zeros((r.give3.shape[0] - end3, LANES), F32))
    wait_y(r.read, r.ysem.at[3])
    partial_hidden = xt_all + r.read[...].reshape(dim, rows)

    def packed_product(left_low, left_high, land):
        both = split(land[...].reshape(half, LANES), 1)
        low = mb(left_low, both)
        high = mb(left_high, both)
        lane2 = lax.broadcasted_iota(jnp.int32, low.shape, 1) % LANES
        picked = jnp.where(lane2 < HEAD, low, high)
        return (picked[:, :LANES] + picked[:, LANES:]).T

    rows_wait(r.land1, r.rsem.at[2])
    far_sum = packed_product(
        r.counts[:, pl.ds(rows, half)], r.counts[:, pl.ds(rows + half, half)], r.land1
    )
    r.mean[mp] = halves(own + far_sum) * inv_degree
    y_send(lambda peer: r.mean.at[mp], r.mean, r.ysem.at[4], r.ysem.at[5])
    wait_y(r.mean, r.ysem.at[5])

    mean_all = r.mean[...].reshape(dim, rows)
    hid_all = partial_hidden + mm(wl_t, mean_all)
    pre = mm(r.wut[...], hid_all)
    gate = 1.0 / (1.0 + jnp.exp(-pre))
    dpre = r.dact[...] * (gate * (1.0 + pre * (1.0 - gate)))
    r.dmp[...] = mm(r.wlu[...], dpre).reshape(r.dmp.shape)
    y_send(lambda peer: r.dmp.at[peer], r.rdm, r.ysem.at[6], r.ysem.at[7])
    r.dhp[...] = mm(r.w_up[...], dpre).reshape(r.dhp.shape)
    y_send(lambda peer: r.dhp.at[peer], r.rdh, r.ysem.at[8], r.ysem.at[9])
    act = pre * gate
    r.brp[...] = mm(r.wdt[...], act).reshape(r.brp.shape)
    y_send(lambda peer: r.brp.at[peer], r.rbr, r.ysem.at[10], r.ysem.at[11])
    r.rdm[mp] = r.dmp[mp] + r.dmean_ct[...]
    r.rdh[mp] = r.dhp[mp] + r.ct[mp]
    r.hid[...] = hid_all.reshape(r.hid.shape)
    r.rbr[mp] = r.brp[mp] + r.hid[mp]
    put3(0, mt(hid_all, dpre))
    grad_down = mt(act, ct_all)
    for b in range(blocks):
        put3(dim + b * units, grad_down[:, b * LANES : (b + 1) * LANES])
    wait_y(r.rdm, r.ysem.at[7])
    dmean = total(r.rdm) * inv_degree

    dtable = halves(mb(split(dmean, 0), r.counts[...]))
    back = jnp.concatenate([dtable[:, rows : rows + half], dtable[:, rows + half :]], 0).T
    r.out2[...] = back.reshape(r.out2.shape)
    for i in order:
        rows_x(i, r.out2, r.mid2, r.rsem.at[3], r.xsem2)
    wait_y(r.rdh, r.ysem.at[9])
    dhid = total(r.rdh)
    r.dx[...] = dhid + dtable[:, :rows]

    dprob = mm(r.fresh[...], dhid)
    a_prob = r.aprob[...]
    dagent = a_prob * (dprob - jnp.sum(a_prob * dprob, 0, keepdims=True)) * scale
    dfresh_part = mt(dagent, xt) + mt(a_prob, dhid)
    no_lanes = jnp.zeros((VN, LANES - HEAD), F32)
    r.give2[...] = jnp.concatenate([dfresh_part, no_lanes], 1).reshape(r.give2.shape)
    group_start(r.give2, r.got2, r.s2)
    wait_x(r.got2, r.s2.at[1])
    r.piece2[...] = total(r.got2)
    z_share(r.piece2, r.gotz2, r.s2)
    for i in order:
        rows_z(i, *rows2)
    grad_local = mt(dhid, mean_all)
    for b in range(blocks):
        put3(base_local + b * HEAD, grad_local[:, b * LANES : (b + 1) * LANES])
    rows3 = r.give3.shape[0] // nxc
    tile3 = rows3 // nz

    def piece3(i):
        return pl.ds(pl.multiple_of(i * rows3, 8), rows3)

    def start3(d):
        peer = x_peer(d)
        send(
            r.give3.at[piece3(peer)], r.got3.at[xc], r.s3.at[0], r.s3.at[1],
            {"graph": z * nxc + peer},
        )

    loop(1, nxc, start3)
    r.got3[xc] = r.give3[piece3(xc), :]
    r.dx[...] = r.dx[...] + mm(r.fresh_t[...], dagent)
    wait_x(r.got3, r.s3.at[1])
    r.piece3[...] = total(r.got3).reshape(nz, tile3, LANES)

    def scatter3(d):
        peer = z_peer(d)
        send(
            r.piece3.at[peer], r.gotz3.at[z], r.s3.at[2], r.s3.at[3],
            {"graph": peer * nxc + xc},
        )

    loop(1, nz, scatter3)
    r.gotz3[z] = r.piece3[z]
    wait_z(r.gotz2, r.s2.at[3])
    r.full2[xc] = total(r.gotz2)
    group_gather(r.full2, r.s2)
    wait_y(r.rbr, r.ysem.at[11])
    r.updated_t[...] = total(r.rbr)
    wait_x(r.full2, r.s2.at[5])
    dfresh = r.full2[...].reshape(VN, LANES)[:, :HEAD]

    dweights = mm(dfresh, r.vt[:HEAD])
    centre = jnp.sum(dfresh * r.attended[...], 1, keepdims=True)
    prob = r.prob[...]
    dscores = prob * (dweights - centre) * scale
    dlatent = mt(dscores, xt)
    r.give4[...] = jnp.concatenate([dlatent, no_lanes], 1).reshape(r.give4.shape)
    group_start(r.give4, r.got4, r.s4)
    dfresh_t = dfresh.T
    dvt = mm(dfresh_t, prob)
    r.dtp[...] = dot(
        r.w_value_t[...], dvt, ((0,), (0,)), lax.Precision.HIGHEST
    ).reshape(r.dtp.shape)
    y_send(lambda peer: r.dtp.at[peer], r.rdt, r.ysem.at[12], r.ysem.at[13])
    r.rdt[mp] = r.dtp[mp] + r.dx[...] + mm(r.latents[...].T, dscores)
    wait_x(r.got4, r.s4.at[1])
    r.piece4[...] = total(r.got4)
    z_share(r.piece4, r.gotz4, r.s4)
    wait_z(r.gotz3, r.s3.at[3])
    r.full3[xc, z] = total(r.gotz3)

    def gather3(d):
        send(
            r.full3.at[xc, z], r.full3.at[xc, z], r.s3.at[4], r.s3.at[5],
            {"graph": z_peer(d) * nxc + xc},
        )

    loop(1, nz, gather3)
    wait_z(r.gotz4, r.s4.at[3])
    r.full4[xc] = total(r.gotz4)
    group_gather(r.full4, r.s4)
    wait(r.full3.at[0, pl.ds(0, nz - 1)], r.s3.at[5])

    def spread3(d):
        send(
            r.full3.at[xc], r.full3.at[xc], r.s3.at[6], r.s3.at[7],
            {"graph": z * nxc + x_peer(d)},
        )

    loop(1, nxc, spread3)
    wait_y(r.rdt, r.ysem.at[13])
    dx = total(r.rdt)

    rows_wait(r.land2, r.rsem.at[5])
    far_back = packed_product(r.st[:, pl.ds(0, half)], r.st[:, pl.ds(half, half)], r.land2)
    r.grad_agents_t[...] = dx + halves(far_back)
    wait_x(r.full4, r.s4.at[5])
    r.grad_latents[...] = (dfresh + r.full4[...].reshape(VN, LANES)[:, :HEAD]) * factor
    wait_x(r.full3, r.s3.at[7])
    sums = r.full3[...].reshape(r.give3.shape)
    r.grad_up[...] = sums[:dim] * factor
    for b in range(blocks):
        cols = pl.ds(b * LANES, LANES)
        r.grad_down[:, cols] = sums[dim + b * units : dim + (b + 1) * units] * factor
        low = base_local + b * HEAD
        r.grad_local_t[:, cols] = sums[low : low + HEAD] * factor
        low = base_prob + b * VN
        r.grad_value_t[:, cols] = mm(dfresh_t, sums[low : low + VN]) * factor

    for give, got_z, full, sems in (
        (r.give1, r.gotz1, r.full1, r.s1),
        (r.give2, r.gotz2, r.full2, r.s2),
        (r.give4, r.gotz4, r.full4, r.s4),
    ):
        wait_x(give, sems.at[0])
        wait_z(got_z, sems.at[2])
        wait_x(full, sems.at[4])
    wait_x(r.got3, r.s3.at[0])
    wait_z(r.gotz3, r.s3.at[2])
    wait(r.full3.at[0, pl.ds(0, nz - 1)], r.s3.at[4])
    wait_x(r.full3, r.s3.at[6])
    for mid, land, base in ((r.mid1, r.land1, 0), (r.mid2, r.land2, 3)):
        wait(mid.at[:, pl.ds(0, nxc - 1)], r.rsem.at[base])
        wait(land.at[pl.ds(0, nz - 1)], r.rsem.at[base + 1])
    wait_y(r.wlt, r.ysem.at[0])
    for i, ref in enumerate((r.read, r.mean, r.rdm, r.rdh, r.rbr, r.rdt)):
        wait_y(ref, r.ysem.at[2 + 2 * i])


def store(*refs):
    count = len(refs) // 2
    sems = refs[-1]
    copies = [
        pltpu.make_async_copy(refs[i], refs[count + i], sems.at[i]) for i in range(count)
    ]
    for copy in copies:
        copy.start()
    for copy in copies:
        copy.wait()


def on_device(
    nz, agents, latents, w_local, w_value, w_up, w_down, neighbours, degree, send_rows, cotangent
):
    rows, dim = agents.shape
    ng = lax.axis_size("graph")
    nmp = lax.axis_size("mp")
    nxc = ng // nz
    units = w_up.shape[1]
    inputs = dict(
        agents=agents,
        latents=latents,
        w_local_t=w_local.T,
        w_value_t=w_value.T,
        w_up=w_up,
        w_down=w_down,
        neighbours_t=neighbours.T,
        degree=degree.reshape(1, rows),
        sends=send_rows[0].T,
        cotangent=cotangent,
    )
    outs = dict(
        updated_t=(HEAD, rows),
        grad_agents_t=(HEAD, rows),
        grad_latents=(VN, HEAD),
        grad_local_t=(HEAD, dim),
        grad_value_t=(HEAD, dim),
        grad_up=(dim, units),
        grad_down=(units, dim),
    )
    half = ng * 8
    blocks = dim // LANES
    step = 8 * nz
    need = (dim + blocks * (units + HEAD + VN)) // nxc
    rows3 = -(-need // step) * step
    rows1 = VN // nxc
    vmem = lambda *shape: pltpu.VMEM(shape, F32)
    dma = lambda n: pltpu.SemaphoreType.DMA((n,))
    scratch = dict(
        xt2=pltpu.VMEM((2 * HEAD, rows), BF16),
        vt=vmem(2 * HEAD, rows),
        st=pltpu.VMEM((rows, 2 * half), BF16),
        counts=pltpu.VMEM((rows, rows + 2 * half), BF16),
        nbm=pltpu.VMEM((rows, SLOTS), jnp.int32),
        weights=vmem(VN, rows),
        prob=vmem(VN, rows),
        aprob=vmem(VN, rows),
        attended=vmem(VN, HEAD),
        fresh=vmem(VN, HEAD),
        fresh_t=vmem(HEAD, VN),
        dact=vmem(units, rows),
        wut=vmem(units, dim),
        wdt=vmem(dim, units),
        wlt=vmem(nmp, HEAD, dim),
        wl=vmem(nmp, HEAD, dim),
        wlu=vmem(dim, units),
        dmean_ct=vmem(HEAD, rows),
        dx=vmem(HEAD, rows),
        xt=vmem(nmp, HEAD, rows),
        ct=vmem(nmp, HEAD, rows),
        read=vmem(nmp, HEAD, rows),
        mean=vmem(nmp, HEAD, rows),
        hid=vmem(nmp, HEAD, rows),
        dmp=vmem(nmp, HEAD, rows),
        rdm=vmem(nmp, HEAD, rows),
        dhp=vmem(nmp, HEAD, rows),
        rdh=vmem(nmp, HEAD, rows),
        brp=vmem(nmp, HEAD, rows),
        rbr=vmem(nmp, HEAD, rows),
        dtp=vmem(nmp, HEAD, rows),
        rdt=vmem(nmp, HEAD, rows),
        give3=vmem(nxc * rows3, LANES),
        got3=vmem(nxc, rows3, LANES),
        piece3=vmem(nz, rows3 // nz, LANES),
        gotz3=vmem(nz, rows3 // nz, LANES),
        full3=vmem(nxc, nz, rows3 // nz, LANES),
        s3=dma(8),
        rsem=dma(6),
        xsem1=dma(4),
        xsem2=dma(4),
        ysem=dma(14),
    )
    for i in (1, 2):
        scratch["out%d" % i] = vmem(nz, nxc, 8, LANES)
        scratch["mid%d" % i] = vmem(nz, nxc, 8, LANES)
        scratch["land%d" % i] = vmem(nz, nxc, 8, LANES)
    for i, n in ((1, rows1), (2, rows1), (4, rows1)):
        scratch["give%d" % i] = vmem(nxc, n, LANES)
        scratch["got%d" % i] = vmem(nxc, n, LANES)
        scratch["piece%d" % i] = vmem(n, LANES)
        scratch["gotz%d" % i] = vmem(nz, n, LANES)
        scratch["full%d" % i] = vmem(nxc, n, LANES)
        scratch["s%d" % i] = dma(6)
    for name, value in inputs.items():
        scratch[name] = pltpu.VMEM(value.shape, value.dtype)
    scratch["lsem"] = dma(len(inputs))
    names = [name + "_hbm" for name in inputs] + list(outs) + list(scratch)
    spec = pl.BlockSpec(memory_space=pltpu.VMEM)
    far_spec = pl.BlockSpec(memory_space=pltpu.HBM)
    result = pl.pallas_call(
        functools.partial(layer, nz, nxc, nmp, rows, dim, names, list(inputs)),
        out_shape=[jax.ShapeDtypeStruct(shape, F32) for shape in outs.values()],
        in_specs=[far_spec] * len(inputs),
        out_specs=[spec] * len(outs),
        scratch_shapes=list(scratch.values()),
        compiler_params=pltpu.CompilerParams(
            collective_id=0, has_side_effects=True, vmem_limit_bytes=62_000_000
        ),
        name="layer",
    )(*inputs.values())
    result = pl.pallas_call(
        store,
        out_shape=[jax.ShapeDtypeStruct(shape, F32) for shape in outs.values()],
        in_specs=[spec] * len(outs),
        out_specs=[far_spec] * len(outs),
        scratch_shapes=[dma(len(outs))],
        compiler_params=pltpu.CompilerParams(vmem_limit_bytes=62_000_000),
        name="store",
    )(*result)
    updated, grad_agents, grad_latents, grad_local, grad_value, grad_up, grad_down = result
    return (
        updated.T,
        grad_agents.T,
        grad_latents,
        grad_local.T,
        grad_value.T,
        grad_up,
        grad_down,
    )


def solution(mesh, nz=16):
    return jax.shard_map(
        functools.partial(on_device, nz),
        mesh=mesh,
        in_specs=(
            P("graph", None),
            P(None, "mp"),
            P(None, "mp"),
            P(None, "mp"),
            P(None, "mp"),
            P("mp", None),
            P("graph", None),
            P("graph"),
            P("graph", None, None),
            P("graph", None),
        ),
        out_specs=(
            P("graph", "mp"),
            P("graph", "mp"),
            P(None, "mp"),
            P(None, "mp"),
            P(None, "mp"),
            P(None, "mp"),
            P("mp", None),
        ),
        check_vma=False,
    )
```

time: 148 us -> 122 us (0.82)
  Pallas kernels: 138 us -> 122 us
  local copies, waits for them, and re-layouts: 9.13 us -> 0 us
    pallas_call x1 -> x2, Pallas kernels: 138 us -> 122 us  [the longest x1 120 us: on_device(): pl.pallas_call(functools.partial(layer, nz, nxc, nmp, rows, dim, names, l...]
    unnamed x18 -> x0, local copies, waits for them, and re-layouts: 5.34 us -> none
    pallas_call x4 -> x0, local copies, waits for them, and re-layouts: 2.85 us -> none  [on_device(): pl.pallas_call(functools.partial(layer, nz, nxc, nmp, rows, dim, names),...]
where the time goes in v2:
time: 122 us
  Pallas kernels  122 us (100%)
    pallas_call x1, Pallas kernels, on_device(): pl.pallas_call(functools.partial(layer, nz, nxc, nmp, rows, dim, names, l...  120 us

profile of v2, /device:TPU:1, one launch (start us, length us, event | category | flops | bytes accessed | tf_op | source)
XLA Modules:
  0.0 122.2 jit_solution(16637237969449407060)
XLA Ops:
  0.6 119.6 %layer.1 = (f32[64,256]{1,0:T(8,128)}, f32[64,256]{1,0:T(8,128)}, f32[64,64]{1,0:T(8,128)}, f32[64,256]{1,0:T(8,128)}, f32[64,256]{1,0:T(8,128)}, /*index=5*/f32[256,128]{1,0:T(8,128)}, f32[128,256]{1,0:T(8,128)}) custom-call(f32[256,256]{1,0:T(8,128)} %refs_0_.1, f32[64,64]{1,0:T(8,128)} %refs_1_.1, f32[64,256]{1,0:T(8,128)} %bitcast.11, ...), custom_call_target="tpu_custom_call" | custom-call | tf_op jit(solution)/shard_map/layer/pallas_call | solution.py:616
  120.2 2.0 %store.1 = (f32[64,256]{1,0:T(8,128)}, f32[64,256]{1,0:T(8,128)}, f32[64,64]{1,0:T(8,128)}, f32[64,256]{1,0:T(8,128)}, f32[64,256]{1,0:T(8,128)}, /*index=5*/f32[256,128]{1,0:T(8,128)}, f32[128,256]{1,0:T(8,128)}) custom-call(f32[64,256]{1,0:T(8,128)} %get-tuple-element.21.refs_0_, f32[64,256]{1,0:T(8,128)} %get-tuple-element.22.refs_1_, ...), custom_call_target="tpu_custom_call" | custom-call | tf_op jit(solution)/shard_map/store/pallas_call | solution.py:627

commit v3 on v2

--- a/solution.py
+++ b/solution.py
@@ -132,6 +132,16 @@
     def wait_z(ref, sem):
         wait(ref.at[pl.ds(0, nz - 1)], sem)
 
+    def put_packed(ref, value):
+        packed = jnp.concatenate([value[: VN // 2], value[VN // 2 :]], 1)
+        n = ref.shape[1]
+        for i in range(ref.shape[0]):
+            ref[i] = packed[i * n : (i + 1) * n]
+
+    def get_packed(ref):
+        packed = jnp.concatenate([ref[i] for i in range(ref.shape[0])], 0)
+        return jnp.concatenate([packed[:, :HEAD], packed[:, HEAD:]], 0)
+
     def total(ref):
         acc = ref[0]
         for i in range(1, ref.shape[0]):
@@ -165,14 +175,29 @@
         loop(1, nxc, go)
         mid[pl.ds(base, 4), xc] = out[pl.ds(base, 4), xc]
 
-    def rows_z(i, mid, land, xr, zs, zr):
+    def rows_z(i, mid, land, via, xr, zs, zr, rs):
         base = lax.rem(zb + nb4 - i, nb4) * 4
         wait(mid.at[pl.ds(0, 4), pl.ds(0, nxc - 1)], xr.at[i])
         for d in range(1 if i == 0 else 0, 4):
             peer = base + lax.rem(zm + d, 4)
-            send(mid.at[peer], land.at[z], zs, zr, {"graph": peer * nxc + xc})
+            device = {"graph": peer * nxc + xc}
+            if i == nb4 // 2 and d == 0:
+                send(mid.at[peer, upper], via, rs.at[0], rs.at[1], {"graph": z_peer(nz - 1) * nxc + xc})
+                send(mid.at[peer, lower], land.at[z, lower], zs, zr, device)
+            else:
+                send(mid.at[peer], land.at[z], zs, zr, device)
         if i == 0:
             land[z] = mid[z]
+
+    lower = pl.ds(0, nxc // 2)
+    upper = pl.ds(nxc // 2, nxc - nxc // 2)
+
+    def rows_relay(mid, land, via, xr, zs, zr, rs):
+        wait(via, rs.at[1])
+        send(
+            via, land.at[z_peer(1), upper], zs, zr,
+            {"graph": z_peer(nz // 2 + 1) * nxc + xc},
+        )
 
     def rows_wait(land, zr):
         wait(land.at[pl.ds(0, nz - 1)], zr)
@@ -186,8 +211,8 @@
         wait(ref.at[pl.ds(0, nmp - 1)], sem)
 
     order = {1: (0,), 2: (1, 0), 4: (2, 1, 3, 0)}[nb4]
-    rows1 = (r.mid1, r.land1, r.xsem1, r.rsem.at[1], r.rsem.at[2])
-    rows2 = (r.mid2, r.land2, r.xsem2, r.rsem.at[4], r.rsem.at[5])
+    rows1 = (r.mid1, r.land1, r.via1, r.xsem1, r.rsem.at[1], r.rsem.at[2], r.vsem1)
+    rows2 = (r.mid2, r.land2, r.via2, r.xsem2, r.rsem2.at[1], r.rsem2.at[2], r.vsem2)
 
     half = ng * 8
     loads["agents"].wait()
@@ -267,6 +292,7 @@
     z_share(r.piece1, r.gotz1, r.s1)
     for i in order:
         rows_z(i, *rows1)
+    rows_relay(*rows1)
     count_part(0)
     loads["w_local_t"].wait()
     r.wlt[mp] = r.w_local_t[...]
@@ -315,14 +341,10 @@
 
     blocks = dim // LANES
     units = r.w_up.shape[1]
-    base_local = dim + blocks * units
-    base_prob = base_local + blocks * HEAD
-    end3 = base_prob + blocks * VN
+    base_prob = dim + blocks * units
     weighted_x = mt(prob, xt_all)
     for b in range(blocks):
         put3(base_prob + b * VN, weighted_x[:, b * LANES : (b + 1) * LANES])
-    if r.give3.shape[0] > end3:
-        put3(end3, jnp.zeros((r.give3.shape[0] - end3, LANES), F32))
     wait_y(r.read, r.ysem.at[3])
     partial_hidden = xt_all + r.read[...].reshape(dim, rows)
 
@@ -347,13 +369,13 @@
     pre = mm(r.wut[...], hid_all)
     gate = 1.0 / (1.0 + jnp.exp(-pre))
     dpre = r.dact[...] * (gate * (1.0 + pre * (1.0 - gate)))
+    r.dhp[...] = mm(r.w_up[...], dpre).reshape(r.dhp.shape)
+    y_send(lambda peer: r.dhp.at[peer], r.rdh, r.ysem2.at[2], r.ysem2.at[3])
     r.dmp[...] = mm(r.wlu[...], dpre).reshape(r.dmp.shape)
-    y_send(lambda peer: r.dmp.at[peer], r.rdm, r.ysem.at[6], r.ysem.at[7])
-    r.dhp[...] = mm(r.w_up[...], dpre).reshape(r.dhp.shape)
-    y_send(lambda peer: r.dhp.at[peer], r.rdh, r.ysem.at[8], r.ysem.at[9])
+    y_send(lambda peer: r.dmp.at[peer], r.rdm, r.ysem2.at[0], r.ysem2.at[1])
     act = pre * gate
     r.brp[...] = mm(r.wdt[...], act).reshape(r.brp.shape)
-    y_send(lambda peer: r.brp.at[peer], r.rbr, r.ysem.at[10], r.ysem.at[11])
+    y_send(lambda peer: r.brp.at[peer], r.rbr, r.ysem2.at[4], r.ysem2.at[5])
     r.rdm[mp] = r.dmp[mp] + r.dmean_ct[...]
     r.rdh[mp] = r.dhp[mp] + r.ct[mp]
     r.hid[...] = hid_all.reshape(r.hid.shape)
@@ -362,38 +384,10 @@
     grad_down = mt(act, ct_all)
     for b in range(blocks):
         put3(dim + b * units, grad_down[:, b * LANES : (b + 1) * LANES])
-    wait_y(r.rdm, r.ysem.at[7])
-    dmean = total(r.rdm) * inv_degree
-
-    dtable = halves(mb(split(dmean, 0), r.counts[...]))
-    back = jnp.concatenate([dtable[:, rows : rows + half], dtable[:, rows + half :]], 0).T
-    r.out2[...] = back.reshape(r.out2.shape)
-    for i in order:
-        rows_x(i, r.out2, r.mid2, r.rsem.at[3], r.xsem2)
-    wait_y(r.rdh, r.ysem.at[9])
-    dhid = total(r.rdh)
-    r.dx[...] = dhid + dtable[:, :rows]
-
-    dprob = mm(r.fresh[...], dhid)
-    a_prob = r.aprob[...]
-    dagent = a_prob * (dprob - jnp.sum(a_prob * dprob, 0, keepdims=True)) * scale
-    dfresh_part = mt(dagent, xt) + mt(a_prob, dhid)
-    no_lanes = jnp.zeros((VN, LANES - HEAD), F32)
-    r.give2[...] = jnp.concatenate([dfresh_part, no_lanes], 1).reshape(r.give2.shape)
-    group_start(r.give2, r.got2, r.s2)
-    wait_x(r.got2, r.s2.at[1])
-    r.piece2[...] = total(r.got2)
-    z_share(r.piece2, r.gotz2, r.s2)
-    for i in order:
-        rows_z(i, *rows2)
-    grad_local = mt(dhid, mean_all)
-    for b in range(blocks):
-        put3(base_local + b * HEAD, grad_local[:, b * LANES : (b + 1) * LANES])
-    rows3 = r.give3.shape[0] // nxc
-    tile3 = rows3 // nz
+    early = r.give3.shape[0] // nxc
 
     def piece3(i):
-        return pl.ds(pl.multiple_of(i * rows3, 8), rows3)
+        return pl.ds(pl.multiple_of(i * early, 8), early)
 
     def start3(d):
         peer = x_peer(d)
@@ -404,58 +398,135 @@
 
     loop(1, nxc, start3)
     r.got3[xc] = r.give3[piece3(xc), :]
-    r.dx[...] = r.dx[...] + mm(r.fresh_t[...], dagent)
+    wait_y(r.rdh, r.ysem2.at[3])
+    dhid = total(r.rdh)
+
+    dprob = mm(r.fresh[...], dhid)
+    a_prob = r.aprob[...]
+    dagent = a_prob * (dprob - jnp.sum(a_prob * dprob, 0, keepdims=True)) * scale
+    dfresh_part = mt(dagent, xt) + mt(a_prob, dhid)
+    put_packed(r.give2, dfresh_part)
+    group_start(r.give2, r.got2, r.s2)
+    grad_local = mt(dhid, mean_all)
+    r.give5[...] = jnp.concatenate(
+        [grad_local[:, b * LANES : (b + 1) * LANES] for b in range(blocks)], 0
+    ).reshape(r.give5.shape)
+    group_start(r.give5, r.got5, r.s5)
+
+    wait_y(r.rdm, r.ysem2.at[1])
+    dmean = total(r.rdm) * inv_degree
+    dtable = halves(mb(split(dmean, 0), r.counts[...]))
+    back = jnp.concatenate([dtable[:, rows : rows + half], dtable[:, rows + half :]], 0).T
+    r.out2[...] = back.reshape(r.out2.shape)
+    for i in order:
+        rows_x(i, r.out2, r.mid2, r.rsem2.at[0], r.xsem2)
+    wait_x(r.got2, r.s2.at[1])
+    r.piece2[...] = total(r.got2)
+    z_share(r.piece2, r.gotz2, r.s2)
     wait_x(r.got3, r.s3.at[1])
-    r.piece3[...] = total(r.got3).reshape(nz, tile3, LANES)
+    tiles_early = early // 8
+    tiles_local = r.piece5.shape[0]
+    tiles = tiles_early + tiles_local
+    r.piece3[...] = total(r.got3).reshape(r.piece3.shape)
 
     def scatter3(d):
         peer = z_peer(d)
-        send(
-            r.piece3.at[peer], r.gotz3.at[z], r.s3.at[2], r.s3.at[3],
-            {"graph": peer * nxc + xc},
-        )
+
+        @pl.when(peer < tiles_early)
+        def _():
+            send(
+                r.piece3.at[peer], r.gotz3.at[z], r.s3.at[2], r.s3.at[3],
+                {"graph": peer * nxc + xc},
+            )
 
     loop(1, nz, scatter3)
-    r.gotz3[z] = r.piece3[z]
+    owner3 = z < tiles_early
+    owner5 = jnp.logical_and(z >= tiles_early, z < tiles)
+    owner = z < tiles
+
+    @pl.when(owner3)
+    def _():
+        r.gotz3[z] = r.piece3[z]
+
+    wait_x(r.got5, r.s5.at[1])
+    r.piece5[...] = total(r.got5).reshape(r.piece5.shape)
+    for j in range(tiles_local):
+
+        @pl.when(z != tiles_early + j)
+        def _():
+            send(
+                r.piece5.at[j], r.gotz5.at[z], r.s5.at[2 + j], r.s5.at[4],
+                {"graph": (tiles_early + j) * nxc + xc},
+            )
+
+        @pl.when(z == tiles_early + j)
+        def _():
+            r.gotz5[z] = r.piece5[j]
+
+    rows_z(order[0], *rows2)
+    r.dx[...] = dhid + dtable[:, :rows] + mm(r.fresh_t[...], dagent)
     wait_z(r.gotz2, r.s2.at[3])
     r.full2[xc] = total(r.gotz2)
     group_gather(r.full2, r.s2)
-    wait_y(r.rbr, r.ysem.at[11])
+
+    def gather3(d):
+        send(
+            r.full3.at[xc, z], r.full3.at[xc, z], r.s3.at[4], r.s3.at[5],
+            {"graph": z_peer(d) * nxc + xc},
+        )
+
+    @pl.when(owner3)
+    def _():
+        wait_z(r.gotz3, r.s3.at[3])
+        r.full3[xc, z] = total(r.gotz3)
+        loop(1, nz, gather3)
+
+    @pl.when(owner5)
+    def _():
+        wait_z(r.gotz5, r.s5.at[4])
+        r.full3[xc, z] = total(r.gotz5)
+        loop(1, nz, gather3)
+
+    for i in order[1:2]:
+        rows_z(i, *rows2)
+    rows_relay(*rows2)
+
+    wait_y(r.rbr, r.ysem2.at[5])
     r.updated_t[...] = total(r.rbr)
     wait_x(r.full2, r.s2.at[5])
-    dfresh = r.full2[...].reshape(VN, LANES)[:, :HEAD]
+    dfresh = get_packed(r.full2)
 
     dweights = mm(dfresh, r.vt[:HEAD])
     centre = jnp.sum(dfresh * r.attended[...], 1, keepdims=True)
     prob = r.prob[...]
     dscores = prob * (dweights - centre) * scale
     dlatent = mt(dscores, xt)
-    r.give4[...] = jnp.concatenate([dlatent, no_lanes], 1).reshape(r.give4.shape)
+    put_packed(r.give4, dlatent)
     group_start(r.give4, r.got4, r.s4)
+    wait_x(r.got4, r.s4.at[1])
+    r.piece4[...] = total(r.got4)
+    z_share(r.piece4, r.gotz4, r.s4)
+    for i in order[2:]:
+        rows_z(i, *rows2)
     dfresh_t = dfresh.T
     dvt = mm(dfresh_t, prob)
     r.dtp[...] = dot(
         r.w_value_t[...], dvt, ((0,), (0,)), lax.Precision.HIGHEST
     ).reshape(r.dtp.shape)
-    y_send(lambda peer: r.dtp.at[peer], r.rdt, r.ysem.at[12], r.ysem.at[13])
+    y_send(lambda peer: r.dtp.at[peer], r.rdt, r.ysem2.at[6], r.ysem2.at[7])
     r.rdt[mp] = r.dtp[mp] + r.dx[...] + mm(r.latents[...].T, dscores)
-    wait_x(r.got4, r.s4.at[1])
-    r.piece4[...] = total(r.got4)
-    z_share(r.piece4, r.gotz4, r.s4)
-    wait_z(r.gotz3, r.s3.at[3])
-    r.full3[xc, z] = total(r.gotz3)
-
-    def gather3(d):
-        send(
-            r.full3.at[xc, z], r.full3.at[xc, z], r.s3.at[4], r.s3.at[5],
-            {"graph": z_peer(d) * nxc + xc},
-        )
-
-    loop(1, nz, gather3)
+
     wait_z(r.gotz4, r.s4.at[3])
     r.full4[xc] = total(r.gotz4)
     group_gather(r.full4, r.s4)
-    wait(r.full3.at[0, pl.ds(0, nz - 1)], r.s3.at[5])
+    @pl.when(owner)
+    def _():
+        wait(r.full3.at[0, pl.ds(0, tiles - 1)], r.s3.at[5])
+
+    @pl.when(jnp.logical_not(owner))
+    def _():
+        wait(r.full3.at[0], r.s3.at[5])
+
 
     def spread3(d):
         send(
@@ -464,24 +535,24 @@
         )
 
     loop(1, nxc, spread3)
-    wait_y(r.rdt, r.ysem.at[13])
+    wait_y(r.rdt, r.ysem2.at[7])
     dx = total(r.rdt)
 
-    rows_wait(r.land2, r.rsem.at[5])
+    rows_wait(r.land2, r.rsem2.at[2])
     far_back = packed_product(r.st[:, pl.ds(0, half)], r.st[:, pl.ds(half, half)], r.land2)
     r.grad_agents_t[...] = dx + halves(far_back)
     wait_x(r.full4, r.s4.at[5])
-    r.grad_latents[...] = (dfresh + r.full4[...].reshape(VN, LANES)[:, :HEAD]) * factor
+    r.grad_latents[...] = (dfresh + get_packed(r.full4)) * factor
     wait_x(r.full3, r.s3.at[7])
-    sums = r.full3[...].reshape(r.give3.shape)
-    r.grad_up[...] = sums[:dim] * factor
+    sums3 = r.full3[:, :tiles_early].reshape(r.give3.shape)
+    sums5 = r.full3[:, tiles_early:].reshape(blocks * HEAD, LANES)
+    r.grad_up[...] = sums3[:dim] * factor
     for b in range(blocks):
         cols = pl.ds(b * LANES, LANES)
-        r.grad_down[:, cols] = sums[dim + b * units : dim + (b + 1) * units] * factor
-        low = base_local + b * HEAD
-        r.grad_local_t[:, cols] = sums[low : low + HEAD] * factor
+        r.grad_down[:, cols] = sums3[dim + b * units : dim + (b + 1) * units] * factor
+        r.grad_local_t[:, cols] = sums5[b * HEAD : (b + 1) * HEAD] * factor
         low = base_prob + b * VN
-        r.grad_value_t[:, cols] = mm(dfresh_t, sums[low : low + VN]) * factor
+        r.grad_value_t[:, cols] = mm(dfresh_t, sums3[low : low + VN]) * factor
 
     for give, got_z, full, sems in (
         (r.give1, r.gotz1, r.full1, r.s1),
@@ -492,15 +563,36 @@
         wait_z(got_z, sems.at[2])
         wait_x(full, sems.at[4])
     wait_x(r.got3, r.s3.at[0])
-    wait_z(r.gotz3, r.s3.at[2])
-    wait(r.full3.at[0, pl.ds(0, nz - 1)], r.s3.at[4])
+    @pl.when(owner3)
+    def _():
+        wait(r.piece3.at[pl.ds(0, tiles_early - 1)], r.s3.at[2])
+
+    @pl.when(jnp.logical_not(owner3))
+    def _():
+        wait(r.piece3, r.s3.at[2])
+
+    for j in range(tiles_local):
+
+        @pl.when(z != tiles_early + j)
+        def _():
+            wait(r.piece5.at[j], r.s5.at[2 + j])
+
+    @pl.when(owner)
+    def _():
+        wait_z(r.gotz3, r.s3.at[4])
+
+    wait_x(r.got5, r.s5.at[0])
     wait_x(r.full3, r.s3.at[6])
-    for mid, land, base in ((r.mid1, r.land1, 0), (r.mid2, r.land2, 3)):
-        wait(mid.at[:, pl.ds(0, nxc - 1)], r.rsem.at[base])
-        wait(land.at[pl.ds(0, nz - 1)], r.rsem.at[base + 1])
+    for mid, land, sems in ((r.mid1, r.land1, r.rsem), (r.mid2, r.land2, r.rsem2)):
+        wait(mid.at[:, pl.ds(0, nxc - 1)], sems.at[0])
+        wait(land.at[pl.ds(0, nz - 1)], sems.at[1])
+    wait(r.via1, r.vsem1.at[0])
+    wait(r.via2, r.vsem2.at[0])
     wait_y(r.wlt, r.ysem.at[0])
-    for i, ref in enumerate((r.read, r.mean, r.rdm, r.rdh, r.rbr, r.rdt)):
+    for i, ref in enumerate((r.read, r.mean)):
         wait_y(ref, r.ysem.at[2 + 2 * i])
+    for i, ref in enumerate((r.rdm, r.rdh, r.rbr, r.rdt)):
+        wait_y(ref, r.ysem2.at[2 * i])
 
 
 def store(*refs):
@@ -546,9 +638,9 @@
     )
     half = ng * 8
     blocks = dim // LANES
-    step = 8 * nz
-    need = (dim + blocks * (units + HEAD + VN)) // nxc
-    rows3 = -(-need // step) * step
+    early = (dim + blocks * (units + VN)) // nxc
+    local = blocks * HEAD // nxc
+    tiles = (early + local) // 8
     rows1 = VN // nxc
     vmem = lambda *shape: pltpu.VMEM(shape, F32)
     dma = lambda n: pltpu.SemaphoreType.DMA((n,))
@@ -585,22 +677,31 @@
         rbr=vmem(nmp, HEAD, rows),
         dtp=vmem(nmp, HEAD, rows),
         rdt=vmem(nmp, HEAD, rows),
-        give3=vmem(nxc * rows3, LANES),
-        got3=vmem(nxc, rows3, LANES),
-        piece3=vmem(nz, rows3 // nz, LANES),
-        gotz3=vmem(nz, rows3 // nz, LANES),
-        full3=vmem(nxc, nz, rows3 // nz, LANES),
+        give3=vmem(nxc * early, LANES),
+        got3=vmem(nxc, early, LANES),
+        piece3=vmem(early // 8, 8, LANES),
+        piece5=vmem(local // 8, 8, LANES),
+        gotz5=vmem(nz, 8, LANES),
+        gotz3=vmem(nz, 8, LANES),
+        full3=vmem(nxc, tiles, 8, LANES),
+        give5=vmem(nxc, local, LANES),
+        got5=vmem(nxc, local, LANES),
+        s5=dma(5),
         s3=dma(8),
-        rsem=dma(6),
+        rsem=dma(3),
+        rsem2=dma(3),
         xsem1=dma(4),
         xsem2=dma(4),
-        ysem=dma(14),
+        ysem=dma(6),
+        ysem2=dma(8),
     )
     for i in (1, 2):
         scratch["out%d" % i] = vmem(nz, nxc, 8, LANES)
         scratch["mid%d" % i] = vmem(nz, nxc, 8, LANES)
         scratch["land%d" % i] = vmem(nz, nxc, 8, LANES)
-    for i, n in ((1, rows1), (2, rows1), (4, rows1)):
+        scratch["via%d" % i] = vmem(nxc - nxc // 2, 8, LANES)
+        scratch["vsem%d" % i] = dma(2)
+    for i, n in ((1, rows1), (2, rows1 // 2), (4, rows1 // 2)):
         scratch["give%d" % i] = vmem(nxc, n, LANES)
         scratch["got%d" % i] = vmem(nxc, n, LANES)
         scratch["piece%d" % i] = vmem(n, LANES)

time: 122 us -> 116 us (0.951)
  Pallas kernels: 122 us -> 115 us
    pallas_call x1, Pallas kernels: 120 us -> 113 us  [on_device(): pl.pallas_call(functools.partial(layer, nz, nxc, nmp, rows, dim, names, l...]
where the time goes in v3:
time: 116 us; the launch traced here: 115 us
  Pallas kernels  115 us (99%)
    pallas_call x1, Pallas kernels, on_device(): pl.pallas_call(functools.partial(layer, nz, nxc, nmp, rows, dim, names, l...  113 us

profile of v3, /device:TPU:1, one launch (start us, length us, event | category | flops | bytes accessed | tf_op | source)
XLA Modules:
  0.0 115.4 jit_solution(1948934240327291878)
XLA Ops:
  0.6 112.8 %layer.1 = (f32[64,256]{1,0:T(8,128)}, f32[64,256]{1,0:T(8,128)}, f32[64,64]{1,0:T(8,128)}, f32[64,256]{1,0:T(8,128)}, f32[64,256]{1,0:T(8,128)}, /*index=5*/f32[256,128]{1,0:T(8,128)}, f32[128,256]{1,0:T(8,128)}) custom-call(f32[256,256]{1,0:T(8,128)} %refs_0_.1, f32[64,64]{1,0:T(8,128)} %refs_1_.1, f32[64,256]{1,0:T(8,128)} %bitcast.11, ...), custom_call_target="tpu_custom_call" | custom-call | tf_op jit(solution)/shard_map/layer/pallas_call | solution.py:717
  113.4 2.0 %store.1 = (f32[64,256]{1,0:T(8,128)}, f32[64,256]{1,0:T(8,128)}, f32[64,64]{1,0:T(8,128)}, f32[64,256]{1,0:T(8,128)}, f32[64,256]{1,0:T(8,128)}, /*index=5*/f32[256,128]{1,0:T(8,128)}, f32[128,256]{1,0:T(8,128)}) custom-call(f32[64,256]{1,0:T(8,128)} %get-tuple-element.21.refs_0_, f32[64,256]{1,0:T(8,128)} %get-tuple-element.22.refs_1_, ...), custom_call_target="tpu_custom_call" | custom-call | tf_op jit(solution)/shard_map/store/pallas_call | solution.py:728

commit v4 on v3

--- a/solution.py
+++ b/solution.py
@@ -516,9 +516,6 @@
     y_send(lambda peer: r.dtp.at[peer], r.rdt, r.ysem2.at[6], r.ysem2.at[7])
     r.rdt[mp] = r.dtp[mp] + r.dx[...] + mm(r.latents[...].T, dscores)
 
-    wait_z(r.gotz4, r.s4.at[3])
-    r.full4[xc] = total(r.gotz4)
-    group_gather(r.full4, r.s4)
     @pl.when(owner)
     def _():
         wait(r.full3.at[0, pl.ds(0, tiles - 1)], r.s3.at[5])
@@ -535,6 +532,9 @@
         )
 
     loop(1, nxc, spread3)
+    wait_z(r.gotz4, r.s4.at[3])
+    r.full4[xc] = total(r.gotz4)
+    group_gather(r.full4, r.s4)
     wait_y(r.rdt, r.ysem2.at[7])
     dx = total(r.rdt)
 

time: 116 us -> 113 us (0.974)
  Pallas kernels: 115 us -> 112 us
    pallas_call x1, Pallas kernels: 113 us -> 110 us  [on_device(): pl.pallas_call(functools.partial(layer, nz, nxc, nmp, rows, dim, names, l...]
where the time goes in v4:
time: 113 us
  Pallas kernels  112 us (99%)
    pallas_call x1, Pallas kernels, on_device(): pl.pallas_call(functools.partial(layer, nz, nxc, nmp, rows, dim, names, l...  110 us

profile of v4, /device:TPU:1, one launch (start us, length us, event | category | flops | bytes accessed | tf_op | source)
XLA Modules:
  0.0 112.8 jit_solution(588979045032977738)
XLA Ops:
  0.6 110.2 %layer.1 = (f32[64,256]{1,0:T(8,128)}, f32[64,256]{1,0:T(8,128)}, f32[64,64]{1,0:T(8,128)}, f32[64,256]{1,0:T(8,128)}, f32[64,256]{1,0:T(8,128)}, /*index=5*/f32[256,128]{1,0:T(8,128)}, f32[128,256]{1,0:T(8,128)}) custom-call(f32[256,256]{1,0:T(8,128)} %refs_0_.1, f32[64,64]{1,0:T(8,128)} %refs_1_.1, f32[64,256]{1,0:T(8,128)} %bitcast.11, ...), custom_call_target="tpu_custom_call" | custom-call | tf_op jit(solution)/shard_map/layer/pallas_call | solution.py:717
  110.8 2.0 %store.1 = (f32[64,256]{1,0:T(8,128)}, f32[64,256]{1,0:T(8,128)}, f32[64,64]{1,0:T(8,128)}, f32[64,256]{1,0:T(8,128)}, f32[64,256]{1,0:T(8,128)}, /*index=5*/f32[256,128]{1,0:T(8,128)}, f32[128,256]{1,0:T(8,128)}) custom-call(f32[64,256]{1,0:T(8,128)} %get-tuple-element.21.refs_0_, f32[64,256]{1,0:T(8,128)} %get-tuple-element.22.refs_1_, ...), custom_call_target="tpu_custom_call" | custom-call | tf_op jit(solution)/shard_map/store/pallas_call | solution.py:728
